TPU v7x, 32 devices: a whole 2x2x4 slice. The times are simulated.
32 devices in a mesh: dp: 8 (over y, x, core), tensor: 4 (over z).
Axes of the slice: x: 2, y: 2, z: 4, core: 2. Of those that a mesh axis runs over, the one named last changes fastest.
Arguments:
- tokens: bfloat16 [32, 200, 768], P(('dp', 'tensor')), may hold values from -6 to 6
- gain_first: float32 [768], replicated, may hold values from 0.25 to 1.75
- qkv_weight: bfloat16 [3, 768, 768], P(None, 'dp', 'tensor'), may hold values from -0.21875 to 0.21875
- out_weight: bfloat16 [768, 768], P('tensor', 'dp'), may hold values from -2 to 2
- gain_second: float32 [768], replicated, may hold values from 0.25 to 1.75
- router_weight: bfloat16 [768, 3], replicated, may hold values from -0.15625 to 0.15625
- expert_in: bfloat16 [3, 768, 3072], P(None, 'dp', 'tensor'), may hold values from -0.21875 to 0.21875
- expert_out: bfloat16 [3, 3072, 768], P(None, 'tensor', 'dp'), may hold values from -0.3125 to 0.3125
- routes: int32 [32, 200, 2], P('dp'), may hold values from 0 to 2, as said below
- slot_index: int32 [32, 200, 2], P('dp'), may hold values from 0 to 525, as said below
- cotangent: bfloat16 [32, 200, 768], P(('dp', 'tensor')), may hold values from -6 to 6
Outputs:
- output: bfloat16 [32, 200, 768], P(('dp', 'tensor'))
- grad_tokens: float32 [32, 200, 768], P(('dp', 'tensor'))
- grad_gain_first: float32 [768], replicated
- grad_qkv_weight: float32 [3, 768, 768], P(None, 'dp', 'tensor')
- grad_out_weight: float32 [768, 768], P('tensor', 'dp')
- grad_gain_second: float32 [768], replicated
- grad_router_weight: float32 [768, 3], replicated
- grad_expert_in: float32 [3, 768, 3072], P(None, 'dp', 'tensor')
- grad_expert_out: float32 [3, 3072, 768], P(None, 'tensor', 'dp')
Inputs may be any that keep to these rules, and one draw needn't show every extreme that they name: `routes`: the 2 entries of a token are different experts. `slot_index`: within the 4 images of one index of dp, slots follow the order of arrival: all first routes in token order, then all second routes; a route at a position below 197 gets the number of earlier such routes to its expert, or 525 when that number is 525 or more (a dropped route); positions 197 and beyond always carry 525. So no two kept routes of one group share an expert and a slot.
All inputs are finite; a program needn't handle non-finite values.
Results may differ from a plain program's by a relative error of at most 0.017.
Values may be sent and summed in bfloat16 or wider, within the bound.
No kernel may reach another device: no remote copies, remote signals or barrier semaphores. Data moves between devices by JAX's collectives and lax.ppermute only.
A program may use at most 128 MiB of HBM per device.

v0:
```python
import math

import jax
import jax.numpy as jnp
from jax import lax
from jax.sharding import PartitionSpec as P

HD = 64
TOPK = 2
VALID = 197
CAP = 525


EPSILON = 1e-06
NEGATIVE = -1e30


def layer_norm(values, gain):
    centered = values - jnp.mean(values, axis=-1, keepdims=True)
    variance = jnp.mean(centered * centered, axis=-1, keepdims=True)
    return centered * lax.rsqrt(variance + EPSILON) * gain


def gelu_exact(values):
    return jax.nn.gelu(values, approximate=False)


def head_split(packed_rows):
    return packed_rows.reshape(packed_rows.shape[:-1] + (packed_rows.shape[-1] // HD, HD))


def masked_scores(query_rows, key_rows, valid_keys, scale):
    raw_scores = (
        jnp.einsum("bqhd,bkhd->bhqk", query_rows, key_rows, preferred_element_type=jnp.float32)
        * scale
    )
    return jnp.where(valid_keys, raw_scores, NEGATIVE)


def attend_forward(first_block, qkv_full, valid_keys, scale):
    packed = jnp.einsum(
        "bsd,cdh->cbsh", first_block, qkv_full, preferred_element_type=jnp.float32
    ).astype(jnp.bfloat16)
    query_rows = head_split(packed[0])
    key_rows = head_split(packed[1])
    value_rows = head_split(packed[2])
    scores = masked_scores(query_rows, key_rows, valid_keys, scale)
    row_max = jnp.max(scores, axis=-1, keepdims=True)
    lifted = jnp.exp(scores - row_max)
    row_total = jnp.sum(lifted, axis=-1, keepdims=True)
    soft_low = (lifted / row_total).astype(jnp.bfloat16)
    mixed_rows = jnp.einsum(
        "bhqk,bkhd->bqhd", soft_low, value_rows, preferred_element_type=jnp.float32
    )
    mixed_rows = mixed_rows.reshape(first_block.shape[:2] + (packed.shape[-1],)).astype(
        jnp.bfloat16
    )
    return (packed, mixed_rows, row_max, row_total)


def attend_backward(
    first_block, packed, grad_block, row_max, row_total, qkv_full, valid_keys, scale
):
    query_rows = head_split(packed[0])
    key_rows = head_split(packed[1])
    value_rows = head_split(packed[2])
    scores = masked_scores(query_rows, key_rows, valid_keys, scale)
    soft = jnp.exp(scores - row_max) / row_total
    soft_low = soft.astype(jnp.bfloat16)
    grad_heads = head_split(grad_block)
    grad_value = jnp.einsum(
        "bhqk,bqhd->bkhd", soft_low, grad_heads, preferred_element_type=jnp.float32
    )
    grad_soft = jnp.einsum(
        "bqhd,bkhd->bhqk", grad_heads, value_rows, preferred_element_type=jnp.float32
    )
    inner = jnp.sum(soft * grad_soft, axis=-1, keepdims=True)
    grad_scores = (soft * (grad_soft - inner)).astype(jnp.bfloat16)
    grad_query = (
        jnp.einsum("bhqk,bkhd->bqhd", grad_scores, key_rows, preferred_element_type=jnp.float32)
        * scale
    )
    grad_key = (
        jnp.einsum("bhqk,bqhd->bkhd", grad_scores, query_rows, preferred_element_type=jnp.float32)
        * scale
    )
    flat_shape = first_block.shape[:2] + (packed.shape[-1],)
    grad_packed = jnp.stack(
        [
            grad_query.reshape(flat_shape),
            grad_key.reshape(flat_shape),
            grad_value.reshape(flat_shape),
        ]
    ).astype(jnp.bfloat16)
    grad_weight_part = jnp.einsum(
        "bsd,cbsh->cdh", first_block, grad_packed, preferred_element_type=jnp.float32
    )
    grad_first_part = jnp.einsum(
        "cbsh,cdh->bsd", grad_packed, qkv_full, preferred_element_type=jnp.float32
    )
    return (grad_weight_part, grad_first_part)


def zero_row(values):
    return jnp.concatenate([values, jnp.zeros((1,) + values.shape[1:], values.dtype)], axis=0)


def on_device(
    tokens,
    gain_first,
    qkv_weight,
    out_weight,
    gain_second,
    router_weight,
    expert_in,
    expert_out,
    routes,
    slot_index,
    cotangent,
):
    pieces = lax.axis_size("tensor")
    piece_index = lax.axis_index("tensor")
    local_images, seq_len, width = tokens.shape
    images = local_images * pieces
    group_rows = images * seq_len
    experts = expert_in.shape[0]
    capacity = CAP
    scale = float(HD) ** (-0.5)
    block_size = math.gcd(images, 4)
    block_count = images // block_size
    valid_keys = jnp.arange(seq_len) < VALID
    qkv_full, out_full, in_full, outexp_full = (
        lax.all_gather(qkv_weight, "dp", axis=1, tiled=True),
        lax.all_gather(out_weight, "dp", axis=1, tiled=True),
        lax.all_gather(expert_in, "dp", axis=1, tiled=True),
        lax.all_gather(expert_out, "dp", axis=2, tiled=True),
    )
    tokens_wide = tokens.astype(jnp.float32)
    first_local = layer_norm(tokens_wide, gain_first).astype(jnp.bfloat16)
    first_norm = lax.all_gather(first_local, "tensor", axis=0, tiled=True)
    first_blocks = first_norm.reshape(block_count, block_size, seq_len, width)

    def attend(first_block):
        return attend_forward(first_block, qkv_full, valid_keys, scale)

    packed, mixed_rows, row_max, row_total = lax.map(attend, first_blocks)
    mixed_flat = mixed_rows.reshape(images, seq_len, mixed_rows.shape[-1])
    attended_part = jnp.einsum(
        "bsh,hd->bsd", mixed_flat, out_full, preferred_element_type=jnp.float32
    )
    attended = lax.psum_scatter(attended_part, "tensor", scatter_dimension=0, tiled=True)
    residual = tokens_wide + attended
    second_local = layer_norm(residual, gain_second).astype(jnp.bfloat16)
    second_norm = lax.all_gather(second_local, "tensor", axis=0, tiled=True)
    second_flat = second_norm.reshape(group_rows, width)
    logits = jnp.dot(second_flat, router_weight, preferred_element_type=jnp.float32)
    gate_probs = jax.nn.softmax(logits, axis=-1)
    route_flat = routes.reshape(group_rows, TOPK)
    slot_flat = slot_index.reshape(group_rows, TOPK)
    position = jnp.arange(group_rows) % seq_len
    live_mask = (slot_flat < capacity) & (position < VALID)[:, None]
    weight = jnp.where(live_mask, jnp.take_along_axis(gate_probs, route_flat, axis=1), 0.0)
    placed = jnp.where(live_mask, route_flat * capacity + slot_flat, experts * capacity)
    assigned = jnp.arange(group_rows * TOPK, dtype=jnp.int32)
    slot_table = (
        jnp.full((experts * capacity + 1,), group_rows * TOPK, jnp.int32)
        .at[placed.reshape(-1)]
        .set(assigned)
    )
    second_padded = zero_row(second_flat)

    def slot_lookup(expert):
        return jnp.where(live_mask & (route_flat == expert), slot_flat, capacity)

    expert_saved = []
    branch = jnp.zeros((group_rows, width), jnp.float32)
    for expert in range(experts):
        expert_owners = slot_table[expert * capacity : (expert + 1) * capacity]
        expert_entering = second_padded[expert_owners // TOPK]
        expert_pre_act = jnp.dot(
            expert_entering, in_full[expert], preferred_element_type=jnp.float32
        )
        expert_hidden = gelu_exact(expert_pre_act).astype(jnp.bfloat16)
        expert_leaving = jnp.dot(
            expert_hidden, outexp_full[expert], preferred_element_type=jnp.float32
        )
        saved_parts = (
            expert_owners,
            expert_entering,
            expert_pre_act,
            expert_hidden,
            expert_leaving,
        )
        expert_saved.append(saved_parts)
        leaving_padded = zero_row(saved_parts[4])
        lookup = slot_lookup(expert)
        for column in range(TOPK):
            branch = branch + weight[:, column : column + 1] * leaving_padded[lookup[:, column]]
    branch_local = lax.psum_scatter(
        branch.reshape(images, seq_len, width).astype(jnp.bfloat16),
        "tensor",
        scatter_dimension=0,
        tiled=True,
    ).astype(jnp.float32)
    output = (residual + branch_local).astype(jnp.bfloat16)
    grad_output = cotangent.astype(jnp.float32)
    grad_branch = lax.all_gather(cotangent, "tensor", axis=0, tiled=True).reshape(group_rows, width)
    grad_padded = zero_row(grad_branch)
    weight_padded = zero_row(weight.reshape(-1))
    grad_second = jnp.zeros((group_rows, width), jnp.float32)
    grad_weight = jnp.zeros((group_rows, TOPK), jnp.float32)
    grads_in = []
    grads_outexp = []
    for expert in range(experts):
        owners, entering, pre_act, hidden, leaving = expert_saved[expert]
        incoming = grad_padded[owners // TOPK].astype(jnp.float32)
        grad_leaving = (weight_padded[owners][:, None] * incoming).astype(jnp.bfloat16)
        grads_outexp.append(
            jnp.einsum("cf,cd->fd", hidden, grad_leaving, preferred_element_type=jnp.float32)
        )
        grad_hidden = jnp.einsum(
            "cd,fd->cf", grad_leaving, outexp_full[expert], preferred_element_type=jnp.float32
        )
        grad_pre = jax.vjp(gelu_exact, pre_act)[1](grad_hidden)[0].astype(jnp.bfloat16)
        grads_in.append(
            jnp.einsum("cd,cf->df", entering, grad_pre, preferred_element_type=jnp.float32)
        )
        grad_entering = zero_row(
            jnp.einsum("cf,df->cd", grad_pre, in_full[expert], preferred_element_type=jnp.float32)
        )
        share = zero_row(jnp.sum(incoming * leaving, axis=-1))
        lookup = slot_lookup(expert)
        for column in range(TOPK):
            grad_second = grad_second + grad_entering[lookup[:, column]]
        grad_weight = grad_weight + share[lookup]
    grad_in_all = jnp.stack(grads_in)
    grad_outexp_all = jnp.stack(grads_outexp)
    second_sum, weight_sum = (
        lax.psum_scatter(
            grad_second.reshape(images, seq_len, width), "tensor", scatter_dimension=0, tiled=True
        ),
        lax.psum_scatter(
            grad_weight.reshape(images, seq_len, TOPK), "tensor", scatter_dimension=0, tiled=True
        ),
    )
    start = piece_index * local_images
    probs_local = lax.dynamic_slice_in_dim(
        gate_probs.reshape(images, seq_len, experts), start, local_images, 0
    )
    routes_local = lax.dynamic_slice_in_dim(routes, start, local_images, 0)
    live_local = lax.dynamic_slice_in_dim(
        live_mask.reshape(images, seq_len, TOPK), start, local_images, 0
    )
    grad_gate = jnp.where(live_local, weight_sum, 0.0)
    chosen = routes_local[..., None] == jnp.arange(experts)
    grad_probs = jnp.sum(jnp.where(chosen, grad_gate[..., None], 0.0), axis=-2)
    grad_logits = (
        probs_local * (grad_probs - jnp.sum(probs_local * grad_probs, axis=-1, keepdims=True))
    ).astype(jnp.bfloat16)
    grad_router = jnp.einsum(
        "bsd,bse->de", second_local, grad_logits, preferred_element_type=jnp.float32
    )
    grad_norm_two = second_sum + jnp.einsum(
        "bse,de->bsd", grad_logits, router_weight, preferred_element_type=jnp.float32
    )
    grad_resid_norm, grad_gain_second = jax.vjp(layer_norm, residual, gain_second)[1](grad_norm_two)
    grad_residual = grad_output + grad_resid_norm
    grad_attended = lax.all_gather(grad_residual.astype(jnp.bfloat16), "tensor", axis=0, tiled=True)
    grad_out_weight = jnp.einsum(
        "bsh,bsd->hd", mixed_flat, grad_attended, preferred_element_type=jnp.float32
    )
    grad_mixed = jnp.einsum(
        "bsd,hd->bsh", grad_attended, out_full, preferred_element_type=jnp.float32
    ).astype(jnp.bfloat16)

    def attend_back(block_parts):
        first_block, packed_block, grad_block, max_block, total_block = block_parts
        return attend_backward(
            first_block,
            packed_block,
            grad_block,
            max_block,
            total_block,
            qkv_full,
            valid_keys,
            scale,
        )

    grad_qkv_parts, grad_first_parts = lax.map(
        attend_back,
        (
            first_blocks,
            packed,
            grad_mixed.reshape(block_count, block_size, seq_len, grad_mixed.shape[-1]),
            row_max,
            row_total,
        ),
    )
    grad_qkv_weight = jnp.sum(grad_qkv_parts, axis=0)
    grad_first = lax.psum_scatter(
        grad_first_parts.reshape(images, seq_len, width).astype(jnp.bfloat16),
        "tensor",
        scatter_dimension=0,
        tiled=True,
    ).astype(jnp.float32)
    grad_tokens_norm, grad_gain_first = jax.vjp(layer_norm, tokens_wide, gain_first)[1](grad_first)
    grad_tokens = grad_residual + grad_tokens_norm
    grad_gain_first, grad_gain_second, grad_router = lax.psum(
        (grad_gain_first, grad_gain_second, grad_router), ("dp", "tensor")
    )
    grad_qkv_weight, grad_out_weight, grad_in_all, grad_outexp_all = (
        lax.psum_scatter(grad_qkv_weight, "dp", scatter_dimension=1, tiled=True),
        lax.psum_scatter(grad_out_weight, "dp", scatter_dimension=1, tiled=True),
        lax.psum_scatter(grad_in_all, "dp", scatter_dimension=1, tiled=True),
        lax.psum_scatter(grad_outexp_all, "dp", scatter_dimension=2, tiled=True),
    )
    return (
        output,
        grad_tokens,
        grad_gain_first,
        grad_qkv_weight,
        grad_out_weight,
        grad_gain_second,
        grad_router,
        grad_in_all,
        grad_outexp_all,
    )


def solution(mesh):
    return jax.shard_map(
        on_device,
        mesh=mesh,
        in_specs=(
            P(("dp", "tensor"), None, None),
            P(),
            P(None, "dp", "tensor"),
            P("tensor", "dp"),
            P(),
            P(),
            P(None, "dp", "tensor"),
            P(None, "tensor", "dp"),
            P("dp", None, None),
            P("dp", None, None),
            P(("dp", "tensor"), None, None),
        ),
        out_specs=(
            P(("dp", "tensor"), None, None),
            P(("dp", "tensor"), None, None),
            P(),
            P(None, "dp", "tensor"),
            P("tensor", "dp"),
            P(),
            P(),
            P(None, "dp", "tensor"),
            P(None, "tensor", "dp"),
        ),
        check_vma=False,
    )
```

profile of v0, /device:TPU:0, one launch (start us, length us, event | category | flops | bytes accessed | tf_op | source)
XLA Modules:
  0.0 690.1 jit_solution(4298129574908220937)
XLA Ops:
  12.8 14.6 %all_gather.25 = bf16[3,768,192]{2,0,1:T(4,128)(2,1)S(1)} all-gather(bf16[3,96,192]{2,0,1:T(4,128)(2,1)S(1)} %copy.129), channel_id=1, replica_groups=mesh['dp'=8,'tensor'=4] {'dp'}, dimensions={1}, use_global_device_ids=true | all-gather | bytes 995328 | tf_op jit(solution)/shard_map/all_gather | solution.py:133
  28.4 8.5 %all_gather.26 = bf16[192,768]{0,1:T(8,128)(2,1)S(1)} all-gather(bf16[192,96]{0,1:T(8,128)(2,1)S(1)} %copy.132), channel_id=1, replica_groups=mesh['dp'=8,'tensor'=4] {'dp'}, dimensions={1}, use_global_device_ids=true | all-gather | bytes 331776 | tf_op jit(solution)/shard_map/all_gather | solution.py:134
  37.0 9.8 %all-gather.7.cloned.1.call-done = bf16[4,200,768]{2,1,0:T(8,128)(2,1)} async-done(((bf16[1,200,768]{2,1,0:T(8,128)(2,1)}), bf16[4,200,768]{2,1,0:T(8,128)(2,1)}) %all-gather.7.cloned.1.call-update) | async-done | bytes 1228816 | tf_op jit(solution)/shard_map/all_gather | solution.py:140
  56.7 48.0 %reduce-scatter.15.cloned.1.call-done = f32[1,200,768]{2,1,0:T(8,128)} async-done(((f32[4,200,768]{2,1,0:T(8,128)}), f32[1,200,768]{2,1,0:T(8,128)}) %reduce-scatter.15.cloned.1.call-update) | async-done | bytes 614416 | tf_op jit(solution)/shard_map/reduce_scatter | solution.py:151
  113.0 9.3 %scatter_custom_fusion = s32[1576]{0:T(1024)S(1)} fusion(s32[1600]{0:T(1024)S(1)} %fusion.84, s32[1600]{0:T(1024)S(1)} %iota.37, s32[]{:T(128)} %constant.106.clone.1), kind=kCustom, calls=%fused_computation.275 | custom fusion | bytes 6308 | tf_op jit(solution)/shard_map/scatter | solution.py:168
  126.7 10.5 %all-gather.15.cloned.1.call-done = bf16[4,200,768]{2,1,0:T(8,128)(2,1)} async-done(((bf16[1,200,768]{2,1,0:T(8,128)(2,1)}), bf16[4,200,768]{2,1,0:T(8,128)(2,1)}) %all-gather.15.cloned.1.call-update) | async-done | bytes 1228816 | tf_op jit(solution)/shard_map/all_gather | solution.py:207
  138.6 3.3 gather_fusion.18
  141.9 3.3 gather_fusion.14
  145.2 3.3 gather_fusion.10
  148.5 20.5 %all-gather.9.cloned.1.call-done = bf16[4,200,768]{2,1,0:T(8,128)(2,1)} async-done(((bf16[1,200,768]{2,1,0:T(8,128)(2,1)}), bf16[4,200,768]{2,1,0:T(8,128)(2,1)}) %all-gather.9.cloned.1.call-update) | async-done | bytes 1228816 | tf_op jit(solution)/shard_map/all_gather | solution.py:154
  173.3 3.3 gather_fusion.3
  180.4 13.7 %gather_fusion.24 = f32[1600]{0:T(1024)S(1)} fusion(f32[800,3]{0,1:T(4,128)S(1)} %fusion.77, s32[1600]{0:T(1024)S(1)} %reshape.825), kind=kCustom, calls=%fused_computation.24 | custom fusion | bytes 25600 | tf_op jit(solution)/shard_map/jit(take_along_axis)/gather | solution.py:162
  194.2 3.5 gather_fusion.17
  197.7 6.1 all-gather.11.cloned.1.call-done
  203.8 6.5 multiply_convert_fusion.1
  210.3 29.3 %all-gather.13.cloned.1.call-done = bf16[3,768,768]{1,2,0:T(8,128)(2,1)} async-done(((bf16[3,768,96]{1,2,0:T(8,128)(2,1)}), bf16[3,768,768]{1,2,0:T(8,128)(2,1)}) %all-gather.13.cloned.1.call-update) | async-done | bytes 3538960 | tf_op jit(solution)/shard_map/all_gather | solution.py:136
  239.6 3.4 add_convert_fusion.1
  246.1 3.9 gather_fusion.20
  250.0 3.8 gather_fusion.19
  253.9 3.7 gather_fusion.13
  257.6 6.2 multiply_convert_fusion.2
  269.9 3.8 gather_fusion.16
  273.8 3.8 gather_fusion.15
  277.6 3.8 gather_fusion.9
  281.4 6.2 multiply_convert_fusion.3
  293.7 3.8 gather_fusion.11
  297.6 3.8 gather_fusion.12
  301.4 7.6 %add_add_fusion = f32[800,768]{1,0:T(8,128)} fusion(f32[800,768]{1,0:T(8,128)} %gather_fusion.20, f32[800,768]{1,0:T(8,128)} %gather_fusion.19, f32[800,768]{1,0:T(8,128)} %gather_fusion.16, f32[800,768]{1,0:T(8,128)} %gather_fusion.15, f32[800,768]{1,0:T(8,128)} %gather_fusion.11, f32[800,768]{1,0:T(8,128)} %gather_fusion.12), kind=kLoop, calls=%fused_computation.32 | loop fusion | flops 3072000 | bytes 17203200 | tf_op jit(solution)/shard_map/add | solution.py:234
  312.8 4.1 gather_fusion.8
  316.8 3.8 gather_fusion.7
  323.9 3.8 gather_fusion.5
  327.7 3.8 gather_fusion.4
  333.9 3.8 gather_fusion.2
  337.7 3.8 gather_fusion.1
  342.3 7.4 %add_convert_fusion = bf16[4,200,768]{2,1,0:T(8,128)(2,1)} fusion(f32[4,200,768]{2,1,0:T(8,128)} %bitcast.206, f32[4,200,768]{2,1,0:T(8,128)} %bitcast.207, f32[4,200,768]{2,1,0:T(8,128)} %bitcast.208, f32[4,200,768]{2,1,0:T(8,128)} %bitcast.209, f32[4,200,768]{2,1,0:T(8,128)} %bitcast.210, f32[4,200,768]{2,1,0:T(8,128)} %bitcast.211, ...), kind=kLoop, calls=%fused_computation.33 | loop fusion | flops 7372800 | bytes 15980800 | tf_op jit(solution)/shard_map/convert_element_type | solution.py:200
  355.0 10.0 %gather_fusion.23 = f32[1600]{0:T(1024)} fusion(f32[526]{0:T(1024)S(1)} %pad_maximum_fusion.6, s32[2048]{0:T(1024)S(1)} %pad_clamp_fusion), kind=kCustom, calls=%fused_computation.23 | custom fusion | bytes 19200 | tf_op jit(solution)/shard_map/gather | solution.py:235
  365.1 6.1 gather_fusion.21
  371.4 6.1 gather_fusion.22
  378.1 12.7 %all-reduce.8 = f32[4,200,2]{1,2,0:T(2,128)S(1)} all-reduce(f32[4,200,2]{1,2,0:T(2,128)S(1)} %copy.153), channel_id=5, replica_groups=mesh['dp'=8,'tensor'=4] {'tensor'}, use_global_device_ids=true, to_apply=%region_15.16.clone | all-reduce | flops 1600 | bytes 12800
  398.2 28.1 %all-gather.17.cloned.1.call-done = bf16[4,200,768]{2,1,0:T(8,128)(2,1)} async-done(((bf16[1,200,768]{2,1,0:T(8,128)(2,1)}), bf16[4,200,768]{2,1,0:T(8,128)(2,1)}) %all-gather.17.cloned.1.call-update) | async-done | bytes 1228816 | tf_op jit(solution)/shard_map/all_gather | solution.py:268
  454.2 3.3 pad_maximum_fusion.1
  457.5 11.1 %copy.179 = f32[3,768,768]{1,0,2:T(4,128)} copy(f32[3,768,768]{2,1,0:T(8,128)} %pad_maximum_fusion.1) | data formatting | bytes 14155776
  468.6 8.2 %copy.185 = f32[96,8,3,768]{3,1,2,0:T(8,128)} copy(f32[96,8,3,768]{3,2,1,0:T(4,128)} %bitcast.203) | data formatting | bytes 14155776
  482.0 3.3 pad_maximum_fusion
  488.1 13.5 %reduce-scatter.21.cloned.1.call-done = bf16[1,200,768]{2,1,0:T(8,128)(2,1)} async-done(((bf16[4,200,768]{2,1,0:T(8,128)(2,1)}), bf16[1,200,768]{2,1,0:T(8,128)(2,1)}) %reduce-scatter.21.cloned.1.call-update) | async-done | bytes 307216 | tf_op jit(solution)/shard_map/reduce_scatter | solution.py:300
  504.3 39.5 %all-reduce.9 = (f32[768]{0:T(1024)}, f32[768]{0:T(1024)}, f32[768,3]{0,1:T(4,128)}) all-reduce(f32[768]{0:T(1024)S(1)} %get-tuple-element.110, f32[768]{0:T(1024)S(1)} %get-tuple-element.108, f32[768,3]{0,1:T(4,128)S(1)} %fusion.73), channel_id=1, replica_groups=mesh['dp'=8,'tensor'=4] {'dp','tensor'}, use_global_device_ids=true, to_apply=%region_25.26 | all-reduce | flops 3840 | bytes 30720 | tf_op jit(solution)/shard_map/psum | solution.py:308
  547.8 66.0 %reduce-scatter.29.cloned.1.call-done = f32[96,2304]{1,0:T(8,128)} async-done(((f32[768,2304]{1,0:T(8,128)}), f32[96,2304]{1,0:T(8,128)}) %reduce-scatter.29.cloned.1.call-update) | async-done | bytes 884752
  616.5 66.8 %reduce-scatter.23.cloned.1.call-done = f32[3,96,768]{2,1,0:T(8,128)} async-done(((f32[3,768,768]{2,1,0:T(8,128)}), f32[3,96,768]{2,1,0:T(8,128)}) %reduce-scatter.23.cloned.1.call-update) | async-done | bytes 884752 | tf_op jit(solution)/shard_map/reduce_scatter | solution.py:314
  (381 shorter events, 121.5 us)
Async XLA Ops:
  7.2 172.7 %copy-start = (bf16[768,3]{0,1:T(4,128)(2,1)S(1)}, bf16[768,3]{0,1:T(4,128)(2,1)}, u32[]{:S(2)}) copy-start(bf16[768,3]{0,1:T(4,128)(2,1)} %param.16) | copy-start | bytes 13828
  7.2 39.5 %all-gather.7.cloned.1.call-start = ((), (), s32[]{:S(2)}) async-start(), calls=%async_computation.8 | async-start | bytes 1536000 | tf_op jit(solution)/shard_map/all_gather | solution.py:140
  12.6 92.1 %reduce-scatter.15.cloned.1.call-start = ((), (), s32[]{:S(2)}) async-start(), calls=%async_computation.9 | async-start | bytes 3072000 | tf_op jit(solution)/shard_map/reduce_scatter | solution.py:151
  27.4 21.7 %copy-start.7 = (bf16[3,768,192]{2,0,1:T(4,128)(2,1)}, bf16[3,768,192]{2,0,1:T(4,128)(2,1)S(1)}, u32[]{:S(2)}) copy-start(bf16[3,768,192]{2,0,1:T(4,128)(2,1)S(1)} %all_gather.25) | copy-start | bytes 2654212
  37.0 16.9 %copy-start.12 = (bf16[192,768]{0,1:T(8,128)(2,1)}, bf16[192,768]{0,1:T(8,128)(2,1)S(1)}, u32[]{:S(2)}) copy-start(bf16[192,768]{0,1:T(8,128)(2,1)S(1)} %all_gather.26) | copy-start | bytes 884740
  55.9 48.8 %copy-start.5 = (bf16[1,200,768]{2,1,0:T(8,128)(2,1)S(1)}, bf16[1,200,768]{2,1,0:T(8,128)(2,1)}, u32[]{:S(2)}) copy-start(bf16[1,200,768]{2,1,0:T(8,128)(2,1)} %param.11) | copy-start | bytes 921604
  55.9 50.9 %copy-start.50 = (f32[768]{0:T(1024)S(1)}, f32[768]{0:T(1024)}, u32[]{:S(2)}) copy-start(f32[768]{0:T(1024)} %param.15) | copy-start | bytes 9220
  55.9 81.2 %all-gather.15.cloned.1.call-start = ((), (), s32[]{:S(2)}) async-start(), calls=%async_computation.14 | async-start | bytes 1536000 | tf_op jit(solution)/shard_map/all_gather | solution.py:207
  56.7 112.3 %all-gather.9.cloned.1.call-start = ((), (), s32[]{:S(2)}) async-start(), calls=%async_computation.10 | async-start | bytes 1536000 | tf_op jit(solution)/shard_map/all_gather | solution.py:154
  107.7 96.1 %all-gather.11.cloned.1.call-start = ((), (), s32[]{:S(2)}) async-start(), calls=%async_computation.11 | async-start | bytes 3981312 | tf_op jit(solution)/shard_map/all_gather | solution.py:135
  108.3 131.3 %all-gather.13.cloned.1.call-start = ((), (), s32[]{:S(2)}) async-start(), calls=%async_computation.12 | async-start | bytes 3981312 | tf_op jit(solution)/shard_map/all_gather | solution.py:136
  108.9 283.4 %reduce-scatter.19.cloned.1.call-start = ((), (), s32[]{:S(2)}) async-start(), calls=%async_computation.15 | async-start | bytes 3072000 | tf_op jit(solution)/shard_map/reduce_scatter | solution.py:239
  109.8 16.3 %copy-start.73 = (pred[800]{0:T(1024)(128)(4,1)}, pred[800]{0:T(1024)(128)(4,1)S(1)}, u32[]{:S(2)}) copy-start(pred[800]{0:T(1024)(128)(4,1)S(1)} %fusion.88) | copy-start | bytes 2404
  111.0 27.5 %copy-start.44 = (s32[800,2]{0,1:T(2,128)}, s32[800,2]{0,1:T(2,128)S(1)}, u32[]{:S(2)}) copy-start(s32[800,2]{0,1:T(2,128)S(1)} %reshape.618) | copy-start | bytes 19204
  111.2 27.4 %copy-start.46 = (s32[800,2]{0,1:T(2,128)}, s32[800,2]{0,1:T(2,128)S(1)}, u32[]{:S(2)}) copy-start(s32[800,2]{0,1:T(2,128)S(1)} %reshape.619) | copy-start | bytes 19204
  173.2 30.6 %copy-start.26 = (bf16[525,768]{1,0:T(8,128)(2,1)}, bf16[525,768]{1,0:T(8,128)(2,1)S(1)}, u32[]{:S(2)}) copy-start(bf16[525,768]{1,0:T(8,128)(2,1)S(1)} %gather_fusion.6) | copy-start | bytes 2419204
  197.7 41.9 %copy-start.84 = (f32[525]{0:T(1024)}, f32[525]{0:T(1024)S(1)}, u32[]{:S(2)}) copy-start(f32[525]{0:T(1024)S(1)} %gather_fusion.17) | copy-start | bytes 6304
  197.7 41.8 %copy-start.32 = (bf16[525,768]{1,0:T(8,128)(2,1)S(1)}, bf16[525,768]{1,0:T(8,128)(2,1)}, u32[]{:S(2)}) copy-start(bf16[525,768]{1,0:T(8,128)(2,1)} %gather_fusion.18) | copy-start | bytes 2419204
  257.6 6.2 copy-start.86
  257.6 6.2 copy-start.30
  281.4 6.2 copy-start.88
  281.4 6.2 copy-start.28
  309.1 84.8 %reduce-scatter.17.cloned.1.call-start = ((), (), s32[]{:S(2)}) async-start(), calls=%async_computation.13 | async-start | bytes 1536000 | tf_op jit(solution)/shard_map/reduce_scatter | solution.py:199
  342.3 8.1 %copy-start.62 = (s32[800,2,1]{0,1,2:T(2,128)S(1)}, s32[800,2,1]{0,1,2:T(2,128)}, u32[]{:S(2)}) copy-start(s32[800,2,1]{0,1,2:T(2,128)} %get-tuple-element.139) | copy-start | bytes 19204
  349.8 76.5 %all-gather.17.cloned.1.call-start = ((), (), s32[]{:S(2)}) async-start(), calls=%async_computation.16 | async-start | bytes 1536000 | tf_op jit(solution)/shard_map/all_gather | solution.py:268
  365.1 6.2 copy-start.1
  371.3 20.1 %copy-start.66 = (pred[4,200,2]{1,0,2:T(4,128)(4,1)S(1)}, pred[4,200,2]{1,0,2:T(4,128)(4,1)}, u32[]{:S(2)}) copy-start(pred[4,200,2]{1,0,2:T(4,128)(4,1)} %copy-done.65) | copy-start | bytes 4804
  371.3 20.1 %copy-start.82 = (pred[1,200]{1,0:T(4,128)(4,1)S(1)}, pred[1,200]{1,0:T(4,128)(4,1)}, u32[]{:S(2)}) copy-start(pred[1,200]{1,0:T(4,128)(4,1)} %constant_dynamic-slice_fusion) | copy-start | bytes 604
  371.3 20.9 %copy-start.81 = (s32[200,2]{0,1:T(2,128)S(1)}, s32[200,2]{0,1:T(2,128)}, u32[]{:S(2)}) copy-start(s32[200,2]{0,1:T(2,128)} %dynamic-slice_bitcast_fusion) | copy-start | bytes 4804
  371.3 20.9 %copy-start.4 = (f32[1,200,768]{2,1,0:T(8,128)S(1)}, f32[1,200,768]{2,1,0:T(8,128)}, u32[]{:S(2)}) copy-start(f32[1,200,768]{2,1,0:T(8,128)} %copy-done.3) | copy-start | bytes 1843204
  371.4 20.9 %copy-start.51 = (f32[768]{0:T(1024)S(1)}, f32[768]{0:T(1024)}, u32[]{:S(2)}) copy-start(f32[768]{0:T(1024)} %param.15) | copy-start | bytes 9220
  371.4 20.9 %copy-start.64 = (f32[200]{0:T(256)S(1)}, f32[200]{0:T(256)}, u32[]{:S(2)}) copy-start(f32[200]{0:T(256)} %copy-done.63) | copy-start | bytes 2404
  371.4 20.9 %copy-start.68 = (f32[200]{0:T(256)S(1)}, f32[200]{0:T(256)}, u32[]{:S(2)}) copy-start(f32[200]{0:T(256)} %copy-done.67) | copy-start | bytes 2404
  377.5 16.3 %copy-start.80 = (f32[200]{0:T(256)S(1)}, f32[200]{0:T(256)}, u32[]{:S(2)}) copy-start(f32[200]{0:T(256)} %copy-done.79) | copy-start | bytes 2404
  393.9 32.4 %copy-start.13 = (bf16[192,768]{0,1:T(8,128)(2,1)S(1)}, bf16[192,768]{0,1:T(8,128)(2,1)}, u32[]{:S(2)}) copy-start(bf16[192,768]{0,1:T(8,128)(2,1)} %copy-done.12) | copy-start | bytes 884740
  396.7 31.4 %copy-start.36 = (bf16[1,4,200,192]{2,3,0,1:T(8,128)(2,1)S(1)}, bf16[1,4,200,192]{2,3,0,1:T(8,128)(2,1)}, u32[]{:S(2)}) copy-start(bf16[1,4,200,192]{2,3,0,1:T(8,128)(2,1)} %copy-done.35) | copy-start | bytes 921604
  396.7 31.4 %copy-start.70 = (f32[4,3,200]{2,1,0:T(4,128)S(1)}, f32[4,3,200]{2,1,0:T(4,128)}, u32[]{:S(2)}) copy-start(f32[4,3,200]{2,1,0:T(4,128)} %copy-done.69) | copy-start | bytes 28804
  397.7 88.8 %reduce-scatter.27.cloned.1.call-start = ((), (), s32[]{:S(2)}) async-start(), calls=%async_computation.20 | async-start | bytes 884736
  434.8 66.8 %reduce-scatter.21.cloned.1.call-start = ((), (), s32[]{:S(2)}) async-start(), calls=%async_computation.17 | async-start | bytes 1536000 | tf_op jit(solution)/shard_map/reduce_scatter | solution.py:300
  440.6 105.3 %reduce-scatter.25.cloned.1.call-start = ((), (), s32[]{:S(2)}) async-start(), calls=%async_computation.19 | async-start | bytes 2211840
  449.0 164.9 %reduce-scatter.29.cloned.1.call-start = ((), (), s32[]{:S(2)}) async-start(), calls=%async_computation.21 | async-start | bytes 7962624
  476.8 206.5 %reduce-scatter.23.cloned.1.call-start = ((), (), s32[]{:S(2)}) async-start(), calls=%async_computation.18 | async-start | bytes 7962624 | tf_op jit(solution)/shard_map/reduce_scatter | solution.py:314
  485.3 16.3 %copy-start.6 = (bf16[1,200,768]{2,1,0:T(8,128)(2,1)S(1)}, bf16[1,200,768]{2,1,0:T(8,128)(2,1)}, u32[]{:S(2)}) copy-start(bf16[1,200,768]{2,1,0:T(8,128)(2,1)} %param.11) | copy-start | bytes 921604
  485.3 16.3 %copy-start.43 = (f32[768]{0:T(1024)S(1)}, f32[768]{0:T(1024)}, u32[]{:S(2)}) copy-start(f32[768]{0:T(1024)} %param.12) | copy-start | bytes 9220
  485.3 16.3 %copy-start.53 = (f32[200]{0:T(256)S(1)}, f32[200]{0:T(256)}, u32[]{:S(2)}) copy-start(f32[200]{0:T(256)} %copy-done.52) | copy-start | bytes 2404
  485.3 17.5 %copy-start.78 = (f32[200]{0:T(256)S(1)}, f32[200]{0:T(256)}, u32[]{:S(2)}) copy-start(f32[200]{0:T(256)} %copy-done.77) | copy-start | bytes 2404
  485.3 17.5 %copy-start.72 = (f32[200]{0:T(256)S(1)}, f32[200]{0:T(256)}, u32[]{:S(2)}) copy-start(f32[200]{0:T(256)} %copy-done.71) | copy-start | bytes 2404
  486.3 57.5 %copy-start.10 = (f32[1,200,768]{2,1,0:T(8,128)S(1)}, f32[1,200,768]{2,1,0:T(8,128)}, u32[]{:S(2)}) copy-start(f32[1,200,768]{2,1,0:T(8,128)} %copy-done.9) | copy-start | bytes 1843204
  (69 other events, 158.2 us)
Sparse Core Ops, SparseCore 0:
  12.7 33.9 all-gather.6
  56.0 48.6 reduce-scatter.14
  106.3 30.8 all-gather.14
  138.6 30.3 all-gather.8
  170.7 33.0 all-gather.10
  205.6 33.9 all-gather.12
  309.2 49.5 reduce-scatter.18
  361.1 30.0 reduce-scatter.16
  397.8 28.4 all-gather.16
  435.0 34.0 reduce-scatter.26
  471.5 30.0 reduce-scatter.20
  504.9 39.5 reduce-scatter.24
  548.4 65.4 reduce-scatter.28
  617.8 65.4 reduce-scatter.22
where the time goes:
time: 699 us; the launch traced here: 690 us
  waiting for transfers between devices  301 us (43%)
  local copies, waits for them, and re-layouts  181 us (26%)
  blocking collectives  75.4 us (11%)
  matrix products  73.9 us (11%)
  other arithmetic  42.4 us (6%)
  between operations  15.6 us (2%)
    unnamed x17, waiting for transfers between devices  67.9 us
    reduce_scatter x1, waiting for transfers between devices, on_device(): lax.psum_scatter(grad_in_all, 'dp', scatter_dimension=1, tiled=True)  66.8 us
    reduce_scatter x1, waiting for transfers between devices, on_device(): lax.psum_scatter(attended_part, 'tensor', scatter_dimension=0, tiled=True)  48 us
    unnamed x221, local copies, waits for them, and re-layouts  45.9 us
    psum x1, blocking collectives, on_device(): lax.psum((grad_gain_first, grad_gain_second, grad_router), ('dp', 'tensor'))  39.5 us
    all_gather x1, waiting for transfers between devices, on_device(): lax.all_gather(expert_out, 'dp', axis=2, tiled=True)  29.3 us
    all_gather x1, waiting for transfers between devices, on_device(): lax.all_gather(grad_residual.astype(jnp.bfloat16), 'tensor', axis=0, tile...  28.1 us
    gather x6, local copies, waits for them, and re-layouts, on_device(): leaving_padded[lookup[:, column]]  23.2 us
  transfers between devices with their start and end apart: 14, of which 10 were waited for; matrix products, arithmetic and copies ran while one was open for 28% of the time, Pallas kernels for 0%

commit v1 on v0

v1 whole, which is shorter than its diff:
```python
import functools

import jax
import jax.numpy as jnp
from jax import lax
from jax.experimental import pallas as pl
from jax.experimental.pallas import tpu as pltpu
from jax.sharding import PartitionSpec as P

HD = 64
VALID = 197
CAP = 525
LANES = 128
EPSILON = 1e-06
NEGATIVE = -1e30
F32 = jnp.float32
BF16 = jnp.bfloat16
VMEM_LIMIT = 58 * 1024 * 1024

KEEP = (0, 2, 4, 6)
SEND = (1, 3, 5, 7)


def nn(a, b):
    return lax.dot_general(a, b, (((1,), (0,)), ((), ())), preferred_element_type=F32)


def nt(a, b):
    return lax.dot_general(a, b, (((1,), (1,)), ((), ())), preferred_element_type=F32)


def tn(a, b):
    return lax.dot_general(a, b, (((0,), (0,)), ((), ())), preferred_element_type=F32)


def norm_parts(values):
    centered = values - jnp.mean(values, axis=-1, keepdims=True)
    variance = jnp.mean(centered * centered, axis=-1, keepdims=True)
    inverse = lax.rsqrt(variance + EPSILON)
    return centered * inverse, inverse


def norm_backward(xhat, inverse, grad, gain):
    h = grad * gain
    mean_h = jnp.mean(h, axis=-1, keepdims=True)
    mean_hx = jnp.mean(h * xhat, axis=-1, keepdims=True)
    return inverse * (h - mean_h - xhat * mean_hx)


def shift(x, axis, size, distance):
    return lax.ppermute(x, axis, [(i, i ^ distance) for i in range(size)])


def after(x, *others):
    return lax.optimization_barrier((x,) + others)[0]


def gather_dp(x, size):
    n = x.shape[0]
    if size != 8:
        full = lax.all_gather(x, "dp", axis=1, tiled=True)
        return [(full, 0, 0)]
    half = n // 2
    from_x = shift(x, "dp", size, 2)
    from_y = shift(x, "dp", size, 4)
    low = shift(from_x[:half], "dp", size, 4)
    high = shift(from_y[half:], "dp", size, 2)
    mine = [(x, 0, 0), (from_x, 0, 2), (from_y, 0, 4), (low, 0, 6), (high, half, 6)]
    return mine + [(shift(a, "dp", size, 1), lo, rel ^ 1) for a, lo, rel in mine]


def reduce_dp(keep, send, size):
    if size != 8:
        return lax.psum_scatter(keep[0], "dp", scatter_dimension=1, tiled=True).astype(F32)
    n = keep.shape[1]
    half = n // 2
    arrived = shift(send, "dp", size, 1)
    total = [keep[j].astype(F32) + arrived[j].astype(F32) for j in range(4)]
    far = total[3].astype(BF16)
    low = shift(far[:half], "dp", size, 2).astype(F32)
    high = shift(far[half:], "dp", size, 4).astype(F32)
    to_x = jnp.concatenate([total[1][:half], total[1][half:] + high]).astype(BF16)
    to_y = jnp.concatenate([total[2][:half] + low, total[2][half:]]).astype(BF16)
    from_x = shift(to_x, "dp", size, 2).astype(F32)
    from_y = shift(to_y, "dp", size, 4).astype(F32)
    return total[0] + from_x + from_y


def start_pieces(layout, refs, where, offs, rows, sems, base=0):
    copies = []
    for ref, (lo, count, rel) in zip(refs, layout):
        spot = pl.multiple_of(offs[rel], 16)
        copy = pltpu.make_async_copy(
            ref, where.at[pl.ds(lo, count), pl.ds(spot, rows), :], sems.at[base + len(copies)]
        )
        copy.start()
        copies.append(copy)
    return copies


def attention_forward(layout, rows, count, offs, tokens, gain1, gain2, *rest):
    pieces = rest[:count]
    resid, second, first, qk_out, v_out, mixed_out, weights, sems = rest[count:]
    copies = start_pieces(layout, pieces, weights, offs, rows, sems)
    wide = tokens[...].astype(F32)
    xhat, _ = norm_parts(wide)
    fn = (xhat * gain1[...]).astype(BF16)
    first[...] = fn
    seq = fn.shape[0]
    for copy in copies:
        copy.wait()
    keys = lax.broadcasted_iota(jnp.int32, (seq, seq), 1) < VALID
    groups = weights.shape[0] // 2
    cols = weights.shape[2] // 2
    total = wide
    for g in range(groups):
        qk = nn(fn, weights[2 * g]).astype(BF16)
        v = nn(fn, weights[2 * g + 1])[:, :cols].astype(BF16)
        qk_out[g] = qk
        v_out[g] = v
        mixed = [jnp.zeros((seq, cols), BF16)]
        for h in range(cols // HD):
            q = qk[:, h * HD : (h + 1) * HD]
            k = qk[:, cols + h * HD : cols + (h + 1) * HD]
            s = jnp.where(keys, nt(q, k) * (HD**-0.5), NEGATIVE)
            e = jnp.exp(s - jnp.max(s, axis=-1, keepdims=True))
            p = e / jnp.sum(e, axis=-1, keepdims=True)
            mixed.append(nn(p.astype(BF16), v[:, h * HD : (h + 1) * HD]).astype(BF16))
        mixed = jnp.concatenate(mixed, axis=1)
        mixed_out[g] = mixed
        total = total + nt(mixed, weights[2 * g + 1])
    resid[...] = total
    xhat, _ = norm_parts(total)
    second[...] = (xhat * gain2[...]).astype(BF16)


def gate_softmax(second, router, experts):
    logits = nn(second, router)
    lane = lax.broadcasted_iota(jnp.int32, logits.shape, 1)
    logits = jnp.where(lane < experts, logits, NEGATIVE)
    e = jnp.exp(logits - jnp.max(logits, axis=-1, keepdims=True))
    return e / jnp.sum(e, axis=-1, keepdims=True)


def normal_cdf_pdf(x):
    z = jnp.abs(x) * 0.7071067811865476
    t = 1.0 / (1.0 + 0.3275911 * z)
    poly = t * (
        0.127414796
        + t * (-0.142248368 + t * (0.7107068705 + t * (-0.7265760135 + t * 0.5307027145)))
    )
    bell = jnp.exp(-0.5 * x * x)
    tail = poly * bell
    return jnp.where(x >= 0, 1.0 - tail, tail), bell * 0.3989422804014327


def expert_dgrad(layout, rows, counts, images, offs, router, *rest):
    experts = len(counts)
    sn = rest[:images]
    cot = rest[images : 2 * images]
    live = rest[2 * images]
    at = 2 * images + 1
    pieces = []
    for c in counts:
        pieces.append(rest[at : at + c])
        at += c
    gs_out = rest[at : at + images]
    br_out = rest[at + images : at + 2 * images]
    dpre_out, hw_out = rest[at + 2 * images : at + 2 * images + 2]
    weights, x_all, c_all, gs_acc, br_acc, w_acc, g_acc, sems = rest[at + 2 * images + 2 :]
    copies = []
    base = 0
    for e in range(experts):
        copies.append(start_pieces(layout, pieces[e], weights.at[e], offs, rows, sems, base))
        base += counts[e]
    seq = sn[0].shape[0]
    width = sn[0].shape[1]
    for j in range(images):
        x_all[pl.ds(j * seq, seq), :] = sn[j][...]
        c_all[pl.ds(j * seq, seq), :] = cot[j][...]
    for e in range(experts):
        for copy in copies[e]:
            copy.wait()

        def tile(j, carry):
            here = pl.ds(pl.multiple_of(j * seq, 16), seq)
            x = x_all[here, :]
            lane = lax.broadcasted_iota(jnp.int32, (seq, LANES), 1)
            if e == 0:
                w = gate_softmax(x, router[...], experts) * live[here, :].astype(F32)
                w_acc[here, :] = w
                g_prev = jnp.zeros((seq, LANES), F32)
            else:
                w = w_acc[here, :]
                g_prev = g_acc[here, :]
            we = w[:, e : e + 1]
            pre = nn(x, weights[e, 0])
            gh = nn(c_all[here, :], weights[e, 1])
            cdf, pdf = normal_cdf_pdf(pre)
            hidden = (pre * cdf).astype(BF16).astype(F32)
            g = jnp.sum(hidden * gh, axis=-1, keepdims=True)
            hw = (hidden * we).astype(BF16)
            dpre = (gh * we * (cdf + pre * pdf)).astype(BF16)
            hw_out[e, here, :] = hw
            dpre_out[e, here, :] = dpre
            g_acc[here, :] = jnp.where((lane == e) | (lane == e + 8), g, g_prev)
            branch = nt(hw, weights[e, 1])
            gs = nt(dpre, weights[e, 0])
            if e == 0:
                br_acc[here, :] = branch
                gs_acc[here, :] = gs
            else:
                br_acc[here, :] += branch
                gs_acc[here, :] += gs
            return carry

        lax.fori_loop(0, images, tile, 0)
    for j in range(images):
        here = pl.ds(j * seq, seq)
        gs_out[j][:, :width] = gs_acc[here, :].astype(BF16)
        g = g_acc[here, :]
        lane = lax.broadcasted_iota(jnp.int32, g.shape, 1)
        coarse = g.astype(BF16)
        gs_out[j][:, width:] = jnp.where(lane < 8, coarse.astype(F32), g - coarse.astype(F32)).astype(BF16)
        br_out[j][...] = br_acc[here, :].astype(BF16)


def put_blocks(acc, outs, blocks, index, offs, rows):
    for which, j, rel in blocks:
        spot = pl.multiple_of(offs[rel], 8)
        outs[which][(j,) + index] = acc[pl.ds(spot, rows), :].astype(BF16)


def expert_wgrad(blocks, n_out, rows, images, offs, *rest):
    sn = rest[:images]
    cot = rest[images : 2 * images]
    dpre, hw = rest[2 * images : 2 * images + 2]
    outs = rest[2 * images + 2 : 2 * images + 2 + n_out]
    acc = rest[-1]
    seq = sn[0].shape[0]
    for m, (left, right) in enumerate(((sn, dpre), (cot, hw))):
        total = None
        for j in range(images):
            part = tn(left[j][...], right[0, pl.ds(j * seq, seq), :])
            total = part if total is None else total + part
        acc[...] = total
        put_blocks(acc, outs, blocks, (m,), offs, rows)


def attention_backward(
    layout, rows, count, blocks, n_out, images, experts, out_rows,
    offs, tokens, gain1, gain2, resid, second, first, qk_in, v_in, mixed_in, live, router, cot, *rest,
):
    gs_in = rest[:images]
    pieces = rest[images : images + count]
    at = images + count
    outs = rest[at : at + n_out]
    grad_tokens, small = rest[at + n_out : at + n_out + 2]
    weights, acc, sems = rest[at + n_out + 2 :]
    copies = start_pieces(layout, pieces, weights, offs, rows, sems)
    width = second.shape[1]
    seq = second.shape[0]
    gs = gs_in[0][...].astype(F32)
    for j in range(1, images):
        gs = gs + gs_in[j][...].astype(F32)
    shares = gs[:, width:]
    gs = gs[:, :width]
    fold = (
        lax.broadcasted_iota(jnp.int32, (LANES, LANES), 0) % 8
        == lax.broadcasted_iota(jnp.int32, (LANES, LANES), 1)
    )
    lane = lax.broadcasted_iota(jnp.int32, shares.shape, 1)
    low_part = jnp.concatenate([shares[:, 8:16], jnp.zeros((seq, LANES - 8), F32)], axis=1)
    shares = jnp.where(lane < experts, shares + low_part, 0.0) * live[...].astype(F32)
    sn = second[...]
    probs = gate_softmax(sn, router[...], experts)
    inner = jnp.sum(probs * shares, axis=-1, keepdims=True)
    grad_logits = (probs * (shares - inner)).astype(BF16)
    grad_router = tn(grad_logits, sn)[:8, :]
    gs = gs + nt(grad_logits, router[...])
    xhat, inverse = norm_parts(resid[...])
    gain2_row = jnp.sum(gs * xhat, axis=0, keepdims=True)
    grad_resid = cot[...].astype(F32) + norm_backward(xhat, inverse, gs, gain2[...])
    ga = grad_resid.astype(BF16)
    fn = first[...]
    keys = lax.broadcasted_iota(jnp.int32, (seq, seq), 1) < VALID
    scale = HD**-0.5
    groups = weights.shape[0] // 2
    cols = weights.shape[2] // 2
    for copy in copies:
        copy.wait()
    grad_first = None
    for g in range(groups):
        gm = nn(ga, weights[2 * g + 1])[:, cols:].astype(BF16)
        qk = qk_in[g]
        v = v_in[g]
        grads_q, grads_k, grads_v = [], [], []
        for h in range(cols // HD):
            q = qk[:, h * HD : (h + 1) * HD]
            k = qk[:, cols + h * HD : cols + (h + 1) * HD]
            gh = gm[:, h * HD : (h + 1) * HD]
            s = jnp.where(keys, nt(q, k) * scale, NEGATIVE)
            e = jnp.exp(s - jnp.max(s, axis=-1, keepdims=True))
            p = e / jnp.sum(e, axis=-1, keepdims=True)
            grads_v.append(tn(p.astype(BF16), gh).astype(BF16))
            gp = nt(gh, v[:, h * HD : (h + 1) * HD])
            ds = (p * (gp - jnp.sum(p * gp, axis=-1, keepdims=True))).astype(BF16)
            grads_q.append((nn(ds, k) * scale).astype(BF16))
            grads_k.append((tn(ds, q) * scale).astype(BF16))
        gqk = jnp.concatenate(grads_q + grads_k, axis=1)
        gv = jnp.concatenate(grads_v + [jnp.zeros((seq, cols), BF16)], axis=1)
        acc[...] = tn(fn, gqk)
        put_blocks(acc, outs, blocks, (2 * g,), offs, rows)
        acc[...] = tn(fn, gv) + tn(ga, mixed_in[g])
        put_blocks(acc, outs, blocks, (2 * g + 1,), offs, rows)
        part = nt(gqk, weights[2 * g]) + nt(gv, weights[2 * g + 1])
        grad_first = part if grad_first is None else grad_first + part
    xhat, inverse = norm_parts(tokens[...].astype(F32))
    gain1_row = jnp.sum(grad_first * xhat, axis=0, keepdims=True)
    result = grad_resid + norm_backward(xhat, inverse, grad_first, gain1[...])
    grad_tokens[...] = result[:out_rows]
    row = lax.broadcasted_iota(jnp.int32, (8, width), 0)
    small[...] = jnp.where(row < experts, grad_router, jnp.where(row == 6, gain1_row, jnp.where(row == 7, gain2_row, 0.0)))


def call(kernel, out_shape, scratch, flops, n_bytes, name, operands, n_any, specs=None):
    total = len(operands)
    in_specs = [pl.BlockSpec(memory_space=pltpu.SMEM)]
    in_specs += [pl.BlockSpec(memory_space=pltpu.VMEM)] * (total - 1 - n_any)
    in_specs += [pl.BlockSpec(memory_space=pl.ANY)] * n_any
    if specs:
        for at, spec in specs.items():
            in_specs[at] = spec
    return pl.pallas_call(
        kernel,
        out_shape=out_shape,
        in_specs=in_specs,
        out_specs=jax.tree.map(lambda _: pl.BlockSpec(memory_space=pltpu.VMEM), out_shape),
        scratch_shapes=scratch,
        compiler_params=pltpu.CompilerParams(vmem_limit_bytes=VMEM_LIMIT),
        cost_estimate=pl.CostEstimate(flops=flops, bytes_accessed=n_bytes, transcendentals=0),
        name=name,
    )(*operands)


def on_device(
    tokens, gain_first, qkv_weight, out_weight, gain_second, router_weight,
    expert_in, expert_out, routes, slot_index, cotangent, *, dp, tensor,
):
    me = lax.axis_index("dp")
    z = lax.axis_index("tensor")
    _, seq_len, width = tokens.shape
    experts, own_rows, ff = expert_in.shape
    cols = qkv_weight.shape[2]
    seq = (seq_len + 15) // 16 * 16
    images = tensor
    split = dp == 8
    rel_count = 8 if split else 1
    rows = width // rel_count
    offs = ((me ^ jnp.arange(8, dtype=jnp.int32)) * rows) if split else jnp.zeros((8,), jnp.int32)
    offs = offs.astype(jnp.int32)
    blocks = (
        [(0, j, r) for j, r in enumerate(KEEP)] + [(1, j, r) for j, r in enumerate(SEND)]
        if split
        else [(0, 0, 0)]
    )
    n_out = 2 if split else 1
    out_lead = 4 if split else 1

    def pad_rows(x):
        return jnp.pad(x, ((0, seq - seq_len), (0, 0)))

    tok = pad_rows(tokens[0])
    cot = pad_rows(cotangent[0])
    g1 = gain_first.reshape(1, width)
    g2 = gain_second.reshape(1, width)
    router = jnp.pad(router_weight, ((0, 0), (0, LANES - experts)))

    own = jnp.stack(
        [
            jnp.concatenate([qkv_weight[0], qkv_weight[1]], axis=1),
            jnp.concatenate([qkv_weight[2], out_weight.T], axis=1),
        ]
    )
    z_pieces = [own] + [shift(own, "tensor", tensor, j) for j in range(1, tensor)]
    z_buffer = jnp.concatenate(z_pieces, axis=0)
    attn_pieces = gather_dp(z_buffer, dp)
    attn_layout = [(lo, a.shape[0], rel) for a, lo, rel in attn_pieces]
    attn_arrays = [a for a, _, _ in attn_pieces]

    cot_go = after(cot, z_buffer)
    cots = [cot] + [shift(cot_go, "tensor", tensor, j) for j in range(1, tensor)]

    token = attn_pieces[4 if split else 0][0]
    expert_arrays = []
    for e in range(experts):
        mine = after(jnp.stack([expert_in[e], expert_out[e].T]), token)
        got = gather_dp(mine, dp)
        expert_layout = [(lo, a.shape[0], rel) for a, lo, rel in got]
        expert_arrays.append([a for a, _, _ in got])
        token = got[4 if split else 0][0]

    groups = tensor
    resid, second, first, qk, v, mixed = call(
        functools.partial(attention_forward, attn_layout, rows, len(attn_arrays)),
        [
            jax.ShapeDtypeStruct((seq, width), F32),
            jax.ShapeDtypeStruct((seq, width), BF16),
            jax.ShapeDtypeStruct((seq, width), BF16),
            jax.ShapeDtypeStruct((groups, seq, 2 * cols), BF16),
            jax.ShapeDtypeStruct((groups, seq, cols), BF16),
            jax.ShapeDtypeStruct((groups, seq, 2 * cols), BF16),
        ],
        [
            pltpu.VMEM((2 * groups, width, 2 * cols), BF16),
            pltpu.SemaphoreType.DMA((len(attn_arrays),)),
        ],
        8_000_000_000, 10_000_000, "attention_forward",
        [offs, tok, g1, g2] + attn_arrays, len(attn_arrays),
    )

    seconds = [second] + [shift(second, "tensor", tensor, j) for j in range(1, tensor)]
    live = (slot_index < CAP) & (jnp.arange(seq_len) < VALID)[None, :, None]
    expert_lane = jnp.arange(LANES)
    live = jnp.any((routes[..., None] == expert_lane) & live[..., None], axis=2).astype(BF16)
    live = jnp.pad(live, ((0, 0), (0, seq - seq_len), (0, 0)))
    live = jnp.concatenate([lax.dynamic_slice_in_dim(live, z ^ j, 1, 0)[0] for j in range(images)], axis=0)

    all_rows = images * seq
    counts = [len(a) for a in expert_arrays]
    flat_experts = [a for group in expert_arrays for a in group]
    outs = call(
        functools.partial(expert_dgrad, expert_layout, rows, counts, images),
        [jax.ShapeDtypeStruct((seq, width + LANES), BF16)] * images
        + [jax.ShapeDtypeStruct((seq, width), BF16)] * images
        + [jax.ShapeDtypeStruct((experts, all_rows, ff), BF16)] * 2,
        [
            pltpu.VMEM((experts, 2, width, ff), BF16),
            pltpu.VMEM((all_rows, width), BF16),
            pltpu.VMEM((all_rows, width), BF16),
            pltpu.VMEM((all_rows, width), F32),
            pltpu.VMEM((all_rows, width), F32),
            pltpu.VMEM((all_rows, LANES), F32),
            pltpu.VMEM((all_rows, LANES), F32),
            pltpu.SemaphoreType.DMA((sum(counts),)),
        ],
        20_000_000_000, 20_000_000, "expert_dgrad",
        [offs, router] + seconds + cots + [live] + flat_experts, len(flat_experts),
    )
    gs_parts = outs[:images]
    branch_parts = outs[images : 2 * images]
    dpre, hw = outs[2 * images :]
    gs_all = [gs_parts[0]] + [shift(gs_parts[j], "tensor", tensor, j) for j in range(1, tensor)]

    grads_in, grads_out = [], []
    vmem = pl.BlockSpec(memory_space=pltpu.VMEM)
    for e in range(experts):
        made = pl.pallas_call(
            functools.partial(expert_wgrad, blocks, n_out, rows, images),
            grid=(1,),
            out_shape=[jax.ShapeDtypeStruct((out_lead, 2, rows, ff), BF16)] * n_out,
            in_specs=[pl.BlockSpec(memory_space=pltpu.SMEM)]
            + [vmem] * (2 * images)
            + [pl.BlockSpec((1, all_rows, ff), functools.partial(lambda e, i: (e, 0, 0), e))] * 2,
            out_specs=[vmem] * n_out,
            scratch_shapes=[pltpu.VMEM((width, ff), F32)],
            compiler_params=pltpu.CompilerParams(vmem_limit_bytes=VMEM_LIMIT),
            cost_estimate=pl.CostEstimate(flops=4_000_000_000, bytes_accessed=8_000_000, transcendentals=0),
            name="expert_wgrad",
        )(offs, *seconds, *cots, dpre, hw)
        summed = reduce_dp(made[0], made[-1], dp)
        grads_in.append(summed[0])
        grads_out.append(summed[1].T)

    outs = call(
        functools.partial(
            attention_backward, attn_layout, rows, len(attn_arrays), blocks, n_out, images, experts, seq_len
        ),
        [jax.ShapeDtypeStruct((out_lead, 2 * groups, rows, 2 * cols), BF16)] * n_out
        + [jax.ShapeDtypeStruct((seq_len, width), F32), jax.ShapeDtypeStruct((8, width), F32)],
        [
            pltpu.VMEM((2 * groups, width, 2 * cols), BF16),
            pltpu.VMEM((width, 2 * cols), F32),
            pltpu.SemaphoreType.DMA((len(attn_arrays),)),
        ],
        16_000_000_000, 16_000_000, "attention_backward",
        [offs, tok, g1, g2, resid, second, first, qk, v, mixed, live[:seq], router, cot]
        + gs_all + attn_arrays,
        len(attn_arrays),
    )
    grad_tokens, small = outs[n_out:]

    tied = lax.optimization_barrier(tuple(branch_parts) + tuple(gs_all))[: len(branch_parts)]
    branch = tied[0].astype(F32)
    for j in range(1, tensor):
        branch = branch + shift(tied[j], "tensor", tensor, j).astype(F32)
    output = (resid + branch)[:seq_len].astype(BF16)

    part = reduce_dp(outs[0], outs[n_out - 1], dp)
    part_low = part.astype(BF16)
    total = part[:2]
    for j in range(1, tensor):
        total = total + shift(part_low[2 * j : 2 * j + 2], "tensor", tensor, j).astype(F32)
    grad_qkv = jnp.stack([total[0, :, :cols], total[0, :, cols:], total[1, :, :cols]])
    grad_out_weight = total[1, :, cols:].T

    if split:
        for axis, size, distance in (("tensor", 4, 1), ("tensor", 4, 2), ("dp", 8, 1), ("dp", 8, 2), ("dp", 8, 4)):
            small = small + shift(small, axis, size, distance)
    else:
        small = lax.psum(small, ("dp", "tensor"))
    return (
        output[None],
        grad_tokens[None],
        small[6],
        grad_qkv,
        grad_out_weight,
        small[7],
        small[:experts].T,
        jnp.stack(grads_in),
        jnp.stack(grads_out),
    )


def solution(mesh):
    sizes = dict(mesh.shape)
    return jax.shard_map(
        functools.partial(on_device, dp=sizes["dp"], tensor=sizes["tensor"]),
        mesh=mesh,
        in_specs=(
            P(("dp", "tensor"), None, None),
            P(),
            P(None, "dp", "tensor"),
            P("tensor", "dp"),
            P(),
            P(),
            P(None, "dp", "tensor"),
            P(None, "tensor", "dp"),
            P("dp", None, None),
            P("dp", None, None),
            P(("dp", "tensor"), None, None),
        ),
        out_specs=(
            P(("dp", "tensor"), None, None),
            P(("dp", "tensor"), None, None),
            P(),
            P(None, "dp", "tensor"),
            P("tensor", "dp"),
            P(),
            P(),
            P(None, "dp", "tensor"),
            P(None, "tensor", "dp"),
        ),
        check_vma=False,
    )
```

time: 699 us -> 366 us (0.52)
  local copies, waits for them, and re-layouts: 181 us -> 10.2 us
  waiting for transfers between devices: 301 us -> 163 us
  starting transfers between devices: 1.21 us -> 94 us
  Pallas kernels: 0 us -> 80.6 us
  blocking collectives: 75.4 us -> 0 us
  matrix products: 73.9 us -> 0 us
  other arithmetic: 42.4 us -> 9.25 us
  between operations: 15.6 us -> 1.96 us
    ppermute x0 -> x79, waiting for transfers between devices: none -> 163 us  [shift(): return lax.ppermute(x, axis, [(i, i ^ distance) for i in range(size)])]
    reduce_scatter x5 -> x0, waiting for transfers between devices: 128 us -> none  [the longest x1 66.8 us: on_device(): lax.psum_scatter(grad_in_all, 'dp', scatter_dimension=1, tiled=True)]
    gather x29 -> x0, local copies, waits for them, and re-layouts: 114 us -> none  [the longest x6 23.2 us: on_device(): leaving_padded[lookup[:, column]]]
    all_gather x6 -> x0, waiting for transfers between devices: 104 us -> none  [the longest x1 29.3 us: on_device(): lax.all_gather(expert_out, 'dp', axis=2, tiled=True)]
    ppermute x0 -> x79, starting transfers between devices: none -> 94 us  [shift(): return lax.ppermute(x, axis, [(i, i ^ distance) for i in range(size)])]
    pallas_call x0 -> x6, Pallas kernels: none -> 80.6 us  [the longest x3 59.8 us: call(): pl.pallas_call(kernel, out_shape=out_shape, in_specs=in_specs, out_specs=...]
    dot_general x32 -> x0, matrix products: 71.4 us -> none  [the longest x3 18.9 us: on_device(): jnp.dot(expert_entering, in_full[expert], preferred_element_type=jnp.floa...]
    unnamed x17 -> x0, waiting for transfers between devices: 67.9 us -> none
  transfers between devices with their start and end apart: 14 -> 79, of which waited for: 10 -> 30; matrix products, arithmetic and copies ran while one was open for 28% -> 3% of each run, Pallas kernels for 0% -> 9%
where the time goes in v1:
time: 366 us; the launch traced here: 359 us
  waiting for transfers between devices  163 us (45%)
  starting transfers between devices  94 us (26%)
  Pallas kernels  80.6 us (22%)
  local copies, waits for them, and re-layouts  10.2 us (3%)
  other arithmetic  9.25 us (3%)
    ppermute x79, waiting for transfers between devices, shift(): return lax.ppermute(x, axis, [(i, i ^ distance) for i in range(size)])  163 us
    ppermute x79, starting transfers between devices, shift(): return lax.ppermute(x, axis, [(i, i ^ distance) for i in range(size)])  94 us
    pallas_call x3, Pallas kernels, call(): pl.pallas_call(kernel, out_shape=out_shape, in_specs=in_specs, out_specs=...  59.8 us
    pallas_call x3, Pallas kernels, on_device(): pl.pallas_call(functools.partial(expert_wgrad, blocks, n_out, rows, image...  20.8 us
  transfers between devices with their start and end apart: 79, of which 30 were waited for; matrix products, arithmetic and copies ran while one was open for 3% of the time, Pallas kernels for 9%

profile of v1, /device:TPU:0, one launch (start us, length us, event | category | flops | bytes accessed | tf_op | source)
XLA Modules:
  0.0 359.2 jit_solution(17001848662420710051)
XLA Ops:
  2.7 3.1 collective-permute-start
  5.8 2.6 collective-permute-start.1
  8.4 3.3 collective-permute-done
  11.7 8.1 %collective-permute-done.1 = bf16[2,96,384]{2,1,0:T(8,128)(2,1)S(1)} collective-permute-done((bf16[2,96,384]{2,1,0:T(8,128)(2,1)S(1)}, bf16[2,96,384]{2,1,0:T(8,128)(2,1)S(1)}, u32[]{:S(2)}, u32[]{:S(2)}) %collective-permute-start.1) | collective-permute-done | bytes 147488 | tf_op jit(solution)/shard_map/ppermute | solution.py:51
  19.9 1.6 collective-permute-start.4
  23.0 9.4 %collective-permute-done.4.rest_2_.rest_6_ = bf16[8,96,384]{2,1,0:T(8,128)(2,1)S(1)} collective-permute-done((bf16[8,96,384]{2,1,0:T(8,128)(2,1)S(1)}, bf16[8,96,384]{2,1,0:T(8,128)(2,1)S(1)}, u32[]{:S(2)}, u32[]{:S(2)}) %collective-permute-start.4) | collective-permute-done | bytes 589856 | tf_op jit(solution)/shard_map/ppermute | solution.py:51
  34.2 2.7 collective-permute-start.17
  36.9 3.4 collective-permute-done.6.rest_4_.rest_8_
  40.9 5.0 %collective-permute-start.16 = (bf16[208,768]{1,0:T(8,128)(2,1)S(1)}, bf16[208,768]{1,0:T(8,128)(2,1)S(1)}, u32[]{:S(2)}, u32[]{:S(2)}) collective-permute-start(bf16[208,768]{1,0:T(8,128)(2,1)S(1)} %pad.20.rest_4_.cot), channel_id=1, source_target_pairs={{0,2},{1,3},{2,0},{3,1},{4,6},{5,7},{6,4},{7,5},{8,10},{9,11},{10,... | collective-permute-start | bytes 958472 | tf_op jit(solution)/shard_map/ppermute | solution.py:51
  45.9 11.5 %collective-permute-start.15 = (bf16[208,768]{1,0:T(8,128)(2,1)S(1)}, bf16[208,768]{1,0:T(8,128)(2,1)S(1)}, u32[]{:S(2)}, u32[]{:S(2)}) collective-permute-start(bf16[208,768]{1,0:T(8,128)(2,1)S(1)} %pad.20.rest_4_.cot), channel_id=1, source_target_pairs={{0,1},{1,0},{2,3},{3,2},{4,5},{5,4},{6,7},{7,6},{8,9},{9,8},{10,11... | collective-permute-start | bytes 958472 | tf_op jit(solution)/shard_map/ppermute | solution.py:51
  57.6 4.7 %collective-permute-done.16.rest_6_ = bf16[208,768]{1,0:T(8,128)(2,1)S(1)} collective-permute-done((bf16[208,768]{1,0:T(8,128)(2,1)S(1)}, bf16[208,768]{1,0:T(8,128)(2,1)S(1)}, u32[]{:S(2)}, u32[]{:S(2)}) %collective-permute-start.16) | collective-permute-done | bytes 319520 | tf_op jit(solution)/shard_map/ppermute | solution.py:51
  63.0 5.1 %collective-permute-done.15.rest_5_ = bf16[208,768]{1,0:T(8,128)(2,1)S(1)} collective-permute-done((bf16[208,768]{1,0:T(8,128)(2,1)S(1)}, bf16[208,768]{1,0:T(8,128)(2,1)S(1)}, u32[]{:S(2)}, u32[]{:S(2)}) %collective-permute-start.15) | collective-permute-done | bytes 319520 | tf_op jit(solution)/shard_map/ppermute | solution.py:51
  70.9 7.3 %collective-permute-done.5.rest_3_.rest_7_ = bf16[4,96,384]{2,1,0:T(8,128)(2,1)} collective-permute-done((bf16[4,96,384]{2,1,0:T(8,128)(2,1)S(1)}, bf16[4,96,384]{2,1,0:T(8,128)(2,1)}, u32[]{:S(2)}, u32[]{:S(2)}) %collective-permute-start.5) | collective-permute-done | bytes 294944 | tf_op jit(solution)/shard_map/ppermute | solution.py:51
  78.9 1.6 collective-permute-start.20
  80.4 2.8 collective-permute-done.28.rest_21_
  88.6 10.5 %attention_forward.1 = (f32[208,768]{1,0:T(8,128)}, bf16[208,768]{1,0:T(8,128)(2,1)}, bf16[208,768]{1,0:T(8,128)(2,1)}, bf16[4,208,384]{2,1,0:T(8,128)(2,1)}, bf...) custom-call(s32[8]{0:T(128)} %xor_multiply_fusion.offs, bf16[208,768]{1,0:T(8,128)(2,1)} %pad.18.tokens, ...), custom_call_target="tpu_custom_call" | custom-call | flops 8000000000 | bytes 10000000 | tf_op jit(solution)/shard_map/attention_forward/pallas_call | solution.py:334
  99.8 3.7 %collective-permute-start.14 = (bf16[208,768]{1,0:T(8,128)(2,1)}, bf16[208,768]{1,0:T(8,128)(2,1)S(1)}, u32[]{:S(2)}, u32[]{:S(2)}) collective-permute-start(bf16[208,768]{1,0:T(8,128)(2,1)} %get-tuple-element.44.rest_0_.second), channel_id=1, source_target_pairs={{0,3},{1,2},{2,1},{3,0},{4,7},{5,6},{6,5},{7,4},{8,11},{9,10},{10,... | collective-permute-start | bytes 958472 | tf_op jit(solution)/shard_map/ppermute | solution.py:51
  104.3 1.6 collective-permute-start.37
  106.4 5.9 %collective-permute-done.14.rest_3_ = bf16[208,768]{1,0:T(8,128)(2,1)S(1)} collective-permute-done((bf16[208,768]{1,0:T(8,128)(2,1)}, bf16[208,768]{1,0:T(8,128)(2,1)S(1)}, u32[]{:S(2)}, u32[]{:S(2)}) %collective-permute-start.14) | collective-permute-done | bytes 319520 | tf_op jit(solution)/shard_map/ppermute | solution.py:51
  113.9 16.3 %collective-permute-done.13.rest_2_ = bf16[208,768]{1,0:T(8,128)(2,1)S(1)} collective-permute-done((bf16[208,768]{1,0:T(8,128)(2,1)}, bf16[208,768]{1,0:T(8,128)(2,1)S(1)}, u32[]{:S(2)}, u32[]{:S(2)}) %collective-permute-start.13) | collective-permute-done | bytes 319520 | tf_op jit(solution)/shard_map/ppermute | solution.py:51
  135.9 2.6 collective-permute-done.39.rest_33_
  140.7 29.6 %expert_dgrad.1 = (bf16[208,896]{1,0:T(8,128)(2,1)}, bf16[208,896]{1,0:T(8,128)(2,1)}, bf16[208,896]{1,0:T(8,128)(2,1)}, bf16[208,896]{1,0:T(8,128)(2,1)}, bf16[...) custom-call(s32[8]{0:T(128)} %xor_multiply_fusion.offs, ...), custom_call_target="tpu_custom_call" | custom-call | flops 20000000000 | bytes 20000000 | tf_op jit(solution)/shard_map/expert_dgrad/pallas_call | solution.py:334
  170.4 3.2 collective-permute-start.46
  174.8 14.2 %collective-permute-done.45.rest_1_ = bf16[208,896]{1,0:T(8,128)(2,1)S(1)} collective-permute-done((bf16[208,896]{1,0:T(8,128)(2,1)}, bf16[208,896]{1,0:T(8,128)(2,1)S(1)}, u32[]{:S(2)}, u32[]{:S(2)}) %collective-permute-start.45) | collective-permute-done | bytes 372768 | tf_op jit(solution)/shard_map/ppermute | solution.py:51
  189.0 10.4 %collective-permute-done.46.rest_2_ = bf16[208,896]{1,0:T(8,128)(2,1)S(1)} collective-permute-done((bf16[208,896]{1,0:T(8,128)(2,1)}, bf16[208,896]{1,0:T(8,128)(2,1)S(1)}, u32[]{:S(2)}, u32[]{:S(2)}) %collective-permute-start.46) | collective-permute-done | bytes 372768 | tf_op jit(solution)/shard_map/ppermute | solution.py:51
  200.2 19.7 %attention_backward.1 = (bf16[4,8,96,384]{3,2,1,0:T(8,128)(2,1)}, bf16[4,8,96,384]{3,2,1,0:T(8,128)(2,1)}, f32[200,768]{1,0:T(8,128)}, f32[8,768]{1,0:T(8,128)}) custom-call(s32[8]{0:T(128)} %xor_multiply_fusion.offs, bf16[208,768]{1,0:T(8,128)(2,1)} %pad.18.tokens, f32[1,768]{1,0:T(1,128)} %reshape.114.gain1, f32[1,768]{1,0:T(1,128)} %reshape.115.gain2, ...), custom_call_target="tpu_custom_call" | custom-call | flops 16000000000 | bytes 16000000 | tf_op jit(solution)/shard_map/attention_backward/pallas_call | solution.py:334
  219.9 7.8 %collective-permute-start.51 = (f32[8,768]{1,0:T(8,128)}, f32[8,768]{1,0:T(8,128)S(1)}, u32[]{:S(2)}, u32[]{:S(2)}) collective-permute-start(f32[8,768]{1,0:T(8,128)} %get-tuple-element.66), channel_id=1, source_target_pairs={{0,1},{1,0},{2,3},{3,2},{4,5},{5,4},{6,7},{7,6},{8,9},{9,8},{10,11... | collective-permute-start | bytes 73736 | tf_op jit(solution)/shard_map/ppermute | solution.py:51
  227.7 2.0 collective-permute-done.51
  230.5 3.0 collective-permute-start.52
  233.5 1.8 collective-permute-done.52
  235.3 6.9 %expert_wgrad.5 = (bf16[4,2,96,768]{3,2,1,0:T(8,128)(2,1)}, bf16[4,2,96,768]{3,2,1,0:T(8,128)(2,1)}) custom-call(s32[8]{0:T(128)} %xor_multiply_fusion.offs, bf16[208,768]{1,0:T(8,128)(2,1)} %get-tuple-element.44.rest_0_.second, bf16[208,768]{1,0:T(8,128)(2,1)} %copy-done.41, bf16[208,768]{1,0:T(8,128)(2,1)} %copy-done.40, bf16[208,768]{1,0:T(8,128)(2,1)} %copy-done.39, ...), custom_call_target="tpu_custom_call" | custom-call | flops 4000000000 | bytes 8000000 | tf_op jit(solution)/shard_map/expert_wgrad/pallas_call | solution.py:458
  244.2 7.0 %expert_wgrad.3 = (bf16[4,2,96,768]{3,2,1,0:T(8,128)(2,1)}, bf16[4,2,96,768]{3,2,1,0:T(8,128)(2,1)}) custom-call(s32[8]{0:T(128)} %xor_multiply_fusion.offs, bf16[208,768]{1,0:T(8,128)(2,1)} %get-tuple-element.44.rest_0_.second, bf16[208,768]{1,0:T(8,128)(2,1)} %copy-done.41, bf16[208,768]{1,0:T(8,128)(2,1)} %copy-done.40, bf16[208,768]{1,0:T(8,128)(2,1)} %copy-done.39, ...), custom_call_target="tpu_custom_call" | custom-call | flops 4000000000 | bytes 8000000 | tf_op jit(solution)/shard_map/expert_wgrad/pallas_call | solution.py:458
  251.2 1.6 collective-permute-start.55
  252.8 7.0 %expert_wgrad.4 = (bf16[4,2,96,768]{3,2,1,0:T(8,128)(2,1)}, bf16[4,2,96,768]{3,2,1,0:T(8,128)(2,1)}) custom-call(s32[8]{0:T(128)} %xor_multiply_fusion.offs, bf16[208,768]{1,0:T(8,128)(2,1)} %get-tuple-element.44.rest_0_.second, bf16[208,768]{1,0:T(8,128)(2,1)} %copy-done.41, bf16[208,768]{1,0:T(8,128)(2,1)} %copy-done.40, bf16[208,768]{1,0:T(8,128)(2,1)} %copy-done.39, ...), custom_call_target="tpu_custom_call" | custom-call | flops 4000000000 | bytes 8000000 | tf_op jit(solution)/shard_map/expert_wgrad/pallas_call | solution.py:458
  259.8 2.0 collective-permute-start.48
  265.5 10.7 %collective-permute-done.48 = bf16[208,768]{1,0:T(8,128)(2,1)S(1)} collective-permute-done((bf16[208,768]{1,0:T(8,128)(2,1)}, bf16[208,768]{1,0:T(8,128)(2,1)S(1)}, u32[]{:S(2)}, u32[]{:S(2)}) %collective-permute-start.48) | collective-permute-done | bytes 319520 | tf_op jit(solution)/shard_map/ppermute | solution.py:51
  276.1 10.8 %collective-permute-done.49 = bf16[208,768]{1,0:T(8,128)(2,1)S(1)} collective-permute-done((bf16[208,768]{1,0:T(8,128)(2,1)}, bf16[208,768]{1,0:T(8,128)(2,1)S(1)}, u32[]{:S(2)}, u32[]{:S(2)}) %collective-permute-start.49) | collective-permute-done | bytes 319520 | tf_op jit(solution)/shard_map/ppermute | solution.py:51
  293.0 1.8 collective-permute-done.75
  296.4 1.6 collective-permute-done.65
  299.8 1.7 collective-permute-done.70
  303.2 4.7 %collective-permute-done.78 = bf16[2,96,768]{2,1,0:T(8,128)(2,1)S(1)} collective-permute-done((bf16[2,96,768]{2,1,0:T(8,128)(2,1)S(1)}, bf16[2,96,768]{2,1,0:T(8,128)(2,1)S(1)}, u32[]{:S(2)}, u32[]{:S(2)}) %collective-permute-start.78) | collective-permute-done | bytes 294944 | tf_op jit(solution)/shard_map/ppermute | solution.py:51
  309.9 4.4 %collective-permute-done.68 = bf16[2,96,768]{2,1,0:T(8,128)(2,1)S(1)} collective-permute-done((bf16[2,96,768]{2,1,0:T(8,128)(2,1)S(1)}, bf16[2,96,768]{2,1,0:T(8,128)(2,1)S(1)}, u32[]{:S(2)}, u32[]{:S(2)}) %collective-permute-start.68) | collective-permute-done | bytes 294944 | tf_op jit(solution)/shard_map/ppermute | solution.py:51
  318.1 8.4 %collective-permute-done.59 = bf16[4,96,384]{2,1,0:T(8,128)(2,1)S(1)} collective-permute-done((bf16[4,96,384]{2,1,0:T(8,128)(2,1)S(1)}, bf16[4,96,384]{2,1,0:T(8,128)(2,1)S(1)}, u32[]{:S(2)}, u32[]{:S(2)}) %collective-permute-start.59) | collective-permute-done | bytes 294944 | tf_op jit(solution)/shard_map/ppermute | solution.py:51
  329.1 11.5 %collective-permute-done.60 = bf16[8,96,384]{2,1,0:T(8,128)(2,1)S(1)} collective-permute-done((bf16[8,96,384]{2,1,0:T(8,128)(2,1)S(1)}, bf16[8,96,384]{2,1,0:T(8,128)(2,1)S(1)}, u32[]{:S(2)}, u32[]{:S(2)}) %collective-permute-start.60) | collective-permute-done | bytes 589856 | tf_op jit(solution)/shard_map/ppermute | solution.py:51
  342.1 3.6 collective-permute-start.61
  345.7 2.4 collective-permute-start.63
  350.2 2.8 collective-permute-done.63
  353.0 4.4 %collective-permute-done.62 = bf16[2,96,384]{2,1,0:T(8,128)(2,1)S(1)} collective-permute-done((bf16[2,96,384]{2,1,0:T(8,128)(2,1)S(1)}, bf16[2,96,384]{2,1,0:T(8,128)(2,1)S(1)}, u32[]{:S(2)}, u32[]{:S(2)}) %collective-permute-start.62) | collective-permute-done | bytes 147488 | tf_op jit(solution)/shard_map/ppermute | solution.py:51
  (302 shorter events, 59.6 us)
Async XLA Ops:
  5.8 14.0 %collective-permute-start.1 = (bf16[2,96,384]{2,1,0:T(8,128)(2,1)S(1)}, bf16[2,96,384]{2,1,0:T(8,128)(2,1)S(1)}, u32[]{:S(2)}, u32[]{:S(2)}) collective-permute-start(bf16[2,96,384]{2,1,0:T(8,128)(2,1)S(1)} %pad_maximum_fusion.15), channel_id=1, source_target_pairs={{0,2},{1,3},{2,0},{3,1},{4,6},{5,7},{6,4},{7,5},{8,10},{9,11},{10,... | collective-permute-start | bytes 442376 | tf_op jit(solution)/shard_map/ppermute | solution.py:51
  8.4 11.4 %collective-permute-start.2 = (bf16[2,96,384]{2,1,0:T(8,128)(2,1)S(1)}, bf16[2,96,384]{2,1,0:T(8,128)(2,1)S(1)}, u32[]{:S(2)}, u32[]{:S(2)}) collective-permute-start(bf16[2,96,384]{2,1,0:T(8,128)(2,1)S(1)} %pad_maximum_fusion.15), channel_id=1, source_target_pairs={{0,3},{1,2},{2,1},{3,0},{4,7},{5,6},{6,5},{7,4},{8,11},{9,10},{10,... | collective-permute-start | bytes 442376 | tf_op jit(solution)/shard_map/ppermute | solution.py:51
  19.9 12.6 %collective-permute-start.4 = (bf16[8,96,384]{2,1,0:T(8,128)(2,1)S(1)}, bf16[8,96,384]{2,1,0:T(8,128)(2,1)S(1)}, u32[]{:S(2)}, u32[]{:S(2)}) collective-permute-start(bf16[8,96,384]{2,1,0:T(8,128)(2,1)S(1)} %constant_dynamic-update-slice_fusion.rest_0_.rest_4_), channel_id=1, source_target_pairs={{0,16},{4,20},{8,24},{12,28},{16,0},{20,4},{24,8},{28,12},{1,17},{... | collective-permute-start | bytes 1769480 | tf_op jit(solution)/shard_map/ppermute | solution.py:51
  21.5 41.3 %collective-permute-start.3 = (bf16[8,96,384]{2,1,0:T(8,128)(2,1)S(1)}, bf16[8,96,384]{2,1,0:T(8,128)(2,1)S(1)}, u32[]{:S(2)}, u32[]{:S(2)}) collective-permute-start(bf16[8,96,384]{2,1,0:T(8,128)(2,1)S(1)} %constant_dynamic-update-slice_fusion.rest_0_.rest_4_), channel_id=1, source_target_pairs={{0,8},{4,12},{8,0},{12,4},{16,24},{20,28},{24,16},{28,20},{1,9},{5... | collective-permute-start | bytes 1769480 | tf_op jit(solution)/shard_map/ppermute | solution.py:51
  34.2 11.8 %collective-permute-start.17 = (bf16[208,768]{1,0:T(8,128)(2,1)S(1)}, bf16[208,768]{1,0:T(8,128)(2,1)S(1)}, u32[]{:S(2)}, u32[]{:S(2)}) collective-permute-start(bf16[208,768]{1,0:T(8,128)(2,1)S(1)} %pad.20.rest_4_.cot), channel_id=1, source_target_pairs={{0,3},{1,2},{2,1},{3,0},{4,7},{5,6},{6,5},{7,4},{8,11},{9,10},{10,... | collective-permute-start | bytes 958472 | tf_op jit(solution)/shard_map/ppermute | solution.py:51
  40.3 17.2 %collective-permute-start.19 = (bf16[2,96,768]{2,1,0:T(8,128)(2,1)S(1)}, bf16[2,96,768]{2,1,0:T(8,128)(2,1)S(1)}, u32[]{:S(2)}, u32[]{:S(2)}) collective-permute-start(bf16[2,96,768]{2,1,0:T(8,128)(2,1)S(1)} %pad_maximum_fusion.4.rest_9_), channel_id=1, source_target_pairs={{0,16},{4,20},{8,24},{12,28},{16,0},{20,4},{24,8},{28,12},{1,17},{... | collective-permute-start | bytes 884744 | tf_op jit(solution)/shard_map/ppermute | solution.py:51
  40.9 21.3 %collective-permute-start.16 = (bf16[208,768]{1,0:T(8,128)(2,1)S(1)}, bf16[208,768]{1,0:T(8,128)(2,1)S(1)}, u32[]{:S(2)}, u32[]{:S(2)}) collective-permute-start(bf16[208,768]{1,0:T(8,128)(2,1)S(1)} %pad.20.rest_4_.cot), channel_id=1, source_target_pairs={{0,2},{1,3},{2,0},{3,1},{4,6},{5,7},{6,4},{7,5},{8,10},{9,11},{10,... | collective-permute-start | bytes 958472 | tf_op jit(solution)/shard_map/ppermute | solution.py:51
  45.9 24.3 %collective-permute-start.7 = (bf16[8,96,384]{2,1,0:T(8,128)(2,1)S(1)}, bf16[8,96,384]{2,1,0:T(8,128)(2,1)S(1)}, u32[]{:S(2)}, u32[]{:S(2)}) collective-permute-start(bf16[8,96,384]{2,1,0:T(8,128)(2,1)S(1)} %constant_dynamic-update-slice_fusion.rest_0_.rest_4_), channel_id=1, source_target_pairs={{0,4},{4,0},{8,12},{12,8},{16,20},{20,16},{24,28},{28,24},{1,5},{5... | collective-permute-start | bytes 1769480 | tf_op jit(solution)/shard_map/ppermute | solution.py:51
  45.9 22.2 %collective-permute-start.15 = (bf16[208,768]{1,0:T(8,128)(2,1)S(1)}, bf16[208,768]{1,0:T(8,128)(2,1)S(1)}, u32[]{:S(2)}, u32[]{:S(2)}) collective-permute-start(bf16[208,768]{1,0:T(8,128)(2,1)S(1)} %pad.20.rest_4_.cot), channel_id=1, source_target_pairs={{0,1},{1,0},{2,3},{3,2},{4,5},{5,4},{6,7},{7,6},{8,9},{9,8},{10,11... | collective-permute-start | bytes 958472 | tf_op jit(solution)/shard_map/ppermute | solution.py:51
  57.5 20.8 %collective-permute-start.9 = (bf16[8,96,384]{2,1,0:T(8,128)(2,1)S(1)}, bf16[8,96,384]{2,1,0:T(8,128)(2,1)S(1)}, u32[]{:S(2)}, u32[]{:S(2)}) collective-permute-start(bf16[8,96,384]{2,1,0:T(8,128)(2,1)S(1)} %collective-permute-done.4.rest_2_.rest_6_), channel_id=1, source_target_pairs={{0,4},{4,0},{8,12},{12,8},{16,20},{20,16},{24,28},{28,24},{1,5},{5... | collective-permute-start | bytes 1769480 | tf_op jit(solution)/shard_map/ppermute | solution.py:51
  63.0 15.9 %collective-permute-start.8 = (bf16[8,96,384]{2,1,0:T(8,128)(2,1)S(1)}, bf16[8,96,384]{2,1,0:T(8,128)(2,1)S(1)}, u32[]{:S(2)}, u32[]{:S(2)}) collective-permute-start(bf16[8,96,384]{2,1,0:T(8,128)(2,1)S(1)} %collective-permute-done.3.rest_1_.rest_5_), channel_id=1, source_target_pairs={{0,4},{4,0},{8,12},{12,8},{16,20},{20,16},{24,28},{28,24},{1,5},{5... | collective-permute-start | bytes 1769480 | tf_op jit(solution)/shard_map/ppermute | solution.py:51
  68.2 10.1 %collective-permute-start.5 = (bf16[4,96,384]{2,1,0:T(8,128)(2,1)S(1)}, bf16[4,96,384]{2,1,0:T(8,128)(2,1)}, u32[]{:S(2)}, u32[]{:S(2)}) collective-permute-start(bf16[4,96,384]{2,1,0:T(8,128)(2,1)S(1)} %slice.469), channel_id=1, source_target_pairs={{0,16},{4,20},{8,24},{12,28},{16,0},{20,4},{24,8},{28,12},{1,17},{... | collective-permute-start | bytes 884744 | tf_op jit(solution)/shard_map/ppermute | solution.py:51
  69.7 9.0 %collective-permute-start.18 = (bf16[2,96,768]{2,1,0:T(8,128)(2,1)S(1)}, bf16[2,96,768]{2,1,0:T(8,128)(2,1)S(1)}, u32[]{:S(2)}, u32[]{:S(2)}) collective-permute-start(bf16[2,96,768]{2,1,0:T(8,128)(2,1)S(1)} %pad_maximum_fusion.4.rest_9_), channel_id=1, source_target_pairs={{0,8},{4,12},{8,0},{12,4},{16,24},{20,28},{24,16},{28,20},{1,9},{5... | collective-permute-start | bytes 884744 | tf_op jit(solution)/shard_map/ppermute | solution.py:51
  70.3 12.9 %collective-permute-start.28 = (bf16[2,96,768]{2,1,0:T(8,128)(2,1)S(1)}, bf16[2,96,768]{2,1,0:T(8,128)(2,1)S(1)}, u32[]{:S(2)}, u32[]{:S(2)}) collective-permute-start(bf16[2,96,768]{2,1,0:T(8,128)(2,1)S(1)} %pad_maximum_fusion.5.rest_19_), channel_id=1, source_target_pairs={{0,16},{4,20},{8,24},{12,28},{16,0},{20,4},{24,8},{28,12},{1,17},{... | collective-permute-start | bytes 884744 | tf_op jit(solution)/shard_map/ppermute | solution.py:51
  85.8 13.3 %collective-permute-start.24 = (bf16[2,96,768]{2,1,0:T(8,128)(2,1)S(1)}, bf16[2,96,768]{2,1,0:T(8,128)(2,1)S(1)}, u32[]{:S(2)}, u32[]{:S(2)}) collective-permute-start(bf16[2,96,768]{2,1,0:T(8,128)(2,1)S(1)} %collective-permute-done.19.rest_11_), channel_id=1, source_target_pairs={{0,4},{4,0},{8,12},{12,8},{16,20},{20,16},{24,28},{28,24},{1,5},{5... | collective-permute-start | bytes 884744 | tf_op jit(solution)/shard_map/ppermute | solution.py:51
  86.3 18.0 %collective-permute-start.23 = (bf16[2,96,768]{2,1,0:T(8,128)(2,1)S(1)}, bf16[2,96,768]{2,1,0:T(8,128)(2,1)S(1)}, u32[]{:S(2)}, u32[]{:S(2)}) collective-permute-start(bf16[2,96,768]{2,1,0:T(8,128)(2,1)S(1)} %collective-permute-done.18.rest_10_), channel_id=1, source_target_pairs={{0,4},{4,0},{8,12},{12,8},{16,20},{20,16},{24,28},{28,24},{1,5},{5... | collective-permute-start | bytes 884744 | tf_op jit(solution)/shard_map/ppermute | solution.py:51
  86.4 19.5 %collective-permute-start.27 = (bf16[2,96,768]{2,1,0:T(8,128)(2,1)S(1)}, bf16[2,96,768]{2,1,0:T(8,128)(2,1)S(1)}, u32[]{:S(2)}, u32[]{:S(2)}) collective-permute-start(bf16[2,96,768]{2,1,0:T(8,128)(2,1)S(1)} %pad_maximum_fusion.5.rest_19_), channel_id=1, source_target_pairs={{0,8},{4,12},{8,0},{12,4},{16,24},{20,28},{24,16},{28,20},{1,9},{5... | collective-permute-start | bytes 884744 | tf_op jit(solution)/shard_map/ppermute | solution.py:51
  86.9 16.6 %collective-permute-start.25 = (bf16[1,96,768]{2,1,0:T(8,128)(2,1)}, bf16[1,96,768]{2,1,0:T(8,128)(2,1)S(1)}, u32[]{:S(2)}, u32[]{:S(2)}) collective-permute-start(bf16[1,96,768]{2,1,0:T(8,128)(2,1)} %collective-permute-done.20.rest_12_), channel_id=1, source_target_pairs={{0,4},{4,0},{8,12},{12,8},{16,20},{20,16},{24,28},{28,24},{1,5},{5... | collective-permute-start | bytes 442376 | tf_op jit(solution)/shard_map/ppermute | solution.py:51
  87.1 16.5 %collective-permute-start.30 = (bf16[1,96,768]{2,1,0:T(8,128)(2,1)S(1)}, bf16[1,96,768]{2,1,0:T(8,128)(2,1)}, u32[]{:S(2)}, u32[]{:S(2)}) collective-permute-start(bf16[1,96,768]{2,1,0:T(8,128)(2,1)S(1)} %slice.474), channel_id=1, source_target_pairs={{0,8},{4,12},{8,0},{12,4},{16,24},{20,28},{24,16},{28,20},{1,9},{5... | collective-permute-start | bytes 442376 | tf_op jit(solution)/shard_map/ppermute | solution.py:51
  99.8 12.5 %collective-permute-start.14 = (bf16[208,768]{1,0:T(8,128)(2,1)}, bf16[208,768]{1,0:T(8,128)(2,1)S(1)}, u32[]{:S(2)}, u32[]{:S(2)}) collective-permute-start(bf16[208,768]{1,0:T(8,128)(2,1)} %get-tuple-element.44.rest_0_.second), channel_id=1, source_target_pairs={{0,3},{1,2},{2,1},{3,0},{4,7},{5,6},{6,5},{7,4},{8,11},{9,10},{10,... | collective-permute-start | bytes 958472 | tf_op jit(solution)/shard_map/ppermute | solution.py:51
  103.6 26.6 %collective-permute-start.13 = (bf16[208,768]{1,0:T(8,128)(2,1)}, bf16[208,768]{1,0:T(8,128)(2,1)S(1)}, u32[]{:S(2)}, u32[]{:S(2)}) collective-permute-start(bf16[208,768]{1,0:T(8,128)(2,1)} %get-tuple-element.44.rest_0_.second), channel_id=1, source_target_pairs={{0,2},{1,3},{2,0},{3,1},{4,6},{5,7},{6,4},{7,5},{8,10},{9,11},{10,... | collective-permute-start | bytes 958472 | tf_op jit(solution)/shard_map/ppermute | solution.py:51
  103.6 26.6 %collective-permute-start.12 = (bf16[208,768]{1,0:T(8,128)(2,1)}, bf16[208,768]{1,0:T(8,128)(2,1)S(1)}, u32[]{:S(2)}, u32[]{:S(2)}) collective-permute-start(bf16[208,768]{1,0:T(8,128)(2,1)} %get-tuple-element.44.rest_0_.second), channel_id=1, source_target_pairs={{0,1},{1,0},{2,3},{3,2},{4,5},{5,4},{6,7},{7,6},{8,9},{9,8},{10,11... | collective-permute-start | bytes 958472 | tf_op jit(solution)/shard_map/ppermute | solution.py:51
  104.3 27.2 %collective-permute-start.37 = (bf16[2,96,768]{2,1,0:T(8,128)(2,1)S(1)}, bf16[2,96,768]{2,1,0:T(8,128)(2,1)S(1)}, u32[]{:S(2)}, u32[]{:S(2)}) collective-permute-start(bf16[2,96,768]{2,1,0:T(8,128)(2,1)S(1)} %pad_maximum_fusion.6.rest_29_), channel_id=1, source_target_pairs={{0,16},{4,20},{8,24},{12,28},{16,0},{20,4},{24,8},{28,12},{1,17},{... | collective-permute-start | bytes 884744 | tf_op jit(solution)/shard_map/ppermute | solution.py:51
  105.9 26.0 %collective-permute-start.36 = (bf16[2,96,768]{2,1,0:T(8,128)(2,1)S(1)}, bf16[2,96,768]{2,1,0:T(8,128)(2,1)S(1)}, u32[]{:S(2)}, u32[]{:S(2)}) collective-permute-start(bf16[2,96,768]{2,1,0:T(8,128)(2,1)S(1)} %pad_maximum_fusion.6.rest_29_), channel_id=1, source_target_pairs={{0,8},{4,12},{8,0},{12,4},{16,24},{20,28},{24,16},{28,20},{1,9},{5... | collective-permute-start | bytes 884744 | tf_op jit(solution)/shard_map/ppermute | solution.py:51
  112.4 19.1 %collective-permute-start.29 = (bf16[1,96,768]{2,1,0:T(8,128)(2,1)S(1)}, bf16[1,96,768]{2,1,0:T(8,128)(2,1)}, u32[]{:S(2)}, u32[]{:S(2)}) collective-permute-start(bf16[1,96,768]{2,1,0:T(8,128)(2,1)S(1)} %slice.473), channel_id=1, source_target_pairs={{0,16},{4,20},{8,24},{12,28},{16,0},{20,4},{24,8},{28,12},{1,17},{... | collective-permute-start | bytes 442376 | tf_op jit(solution)/shard_map/ppermute | solution.py:51
  170.3 18.7 %collective-permute-start.45 = (bf16[208,896]{1,0:T(8,128)(2,1)}, bf16[208,896]{1,0:T(8,128)(2,1)S(1)}, u32[]{:S(2)}, u32[]{:S(2)}) collective-permute-start(bf16[208,896]{1,0:T(8,128)(2,1)} %get-tuple-element.54), channel_id=1, source_target_pairs={{0,1},{1,0},{2,3},{3,2},{4,5},{5,4},{6,7},{7,6},{8,9},{9,8},{10,11... | collective-permute-start | bytes 1118216 | tf_op jit(solution)/shard_map/ppermute | solution.py:51
  170.4 28.9 %collective-permute-start.46 = (bf16[208,896]{1,0:T(8,128)(2,1)}, bf16[208,896]{1,0:T(8,128)(2,1)S(1)}, u32[]{:S(2)}, u32[]{:S(2)}) collective-permute-start(bf16[208,896]{1,0:T(8,128)(2,1)} %get-tuple-element.55), channel_id=1, source_target_pairs={{0,2},{1,3},{2,0},{3,1},{4,6},{5,7},{6,4},{7,5},{8,10},{9,11},{10,... | collective-permute-start | bytes 1118216 | tf_op jit(solution)/shard_map/ppermute | solution.py:51
  173.6 25.7 %collective-permute-start.47 = (bf16[208,896]{1,0:T(8,128)(2,1)}, bf16[208,896]{1,0:T(8,128)(2,1)S(1)}, u32[]{:S(2)}, u32[]{:S(2)}) collective-permute-start(bf16[208,896]{1,0:T(8,128)(2,1)} %get-tuple-element.56), channel_id=1, source_target_pairs={{0,3},{1,2},{2,1},{3,0},{4,7},{5,6},{6,5},{7,4},{8,11},{9,10},{10,... | collective-permute-start | bytes 1118216 | tf_op jit(solution)/shard_map/ppermute | solution.py:51
  219.9 9.8 %collective-permute-start.51 = (f32[8,768]{1,0:T(8,128)}, f32[8,768]{1,0:T(8,128)S(1)}, u32[]{:S(2)}, u32[]{:S(2)}) collective-permute-start(f32[8,768]{1,0:T(8,128)} %get-tuple-element.66), channel_id=1, source_target_pairs={{0,1},{1,0},{2,3},{3,2},{4,5},{5,4},{6,7},{7,6},{8,9},{9,8},{10,11... | collective-permute-start | bytes 73736 | tf_op jit(solution)/shard_map/ppermute | solution.py:51
  242.2 45.7 %collective-permute-start.74 = (bf16[4,2,96,768]{3,2,1,0:T(8,128)(2,1)}, bf16[4,2,96,768]{3,2,1,0:T(8,128)(2,1)S(1)}, u32[]{:S(2)}, u32[]{:S(2)}) collective-permute-start(bf16[4,2,96,768]{3,2,1,0:T(8,128)(2,1)} %get-tuple-element.76), channel_id=1, source_target_pairs={{0,4},{4,0},{8,12},{12,8},{16,20},{20,16},{24,28},{28,24},{1,5},{5... | collective-permute-start | bytes 3538952 | tf_op jit(solution)/shard_map/ppermute | solution.py:51
  251.1 38.5 %collective-permute-start.64 = (bf16[4,2,96,768]{3,2,1,0:T(8,128)(2,1)}, bf16[4,2,96,768]{3,2,1,0:T(8,128)(2,1)S(1)}, u32[]{:S(2)}, u32[]{:S(2)}) collective-permute-start(bf16[4,2,96,768]{3,2,1,0:T(8,128)(2,1)} %get-tuple-element.72), channel_id=1, source_target_pairs={{0,4},{4,0},{8,12},{12,8},{16,20},{20,16},{24,28},{28,24},{1,5},{5... | collective-permute-start | bytes 3538952 | tf_op jit(solution)/shard_map/ppermute | solution.py:51
  251.2 11.6 %collective-permute-start.55 = (f32[8,768]{1,0:T(8,128)S(1)}, f32[8,768]{1,0:T(8,128)S(1)}, u32[]{:S(2)}, u32[]{:S(2)}) collective-permute-start(f32[8,768]{1,0:T(8,128)S(1)} %add.185), channel_id=1, source_target_pairs={{0,16},{4,20},{8,24},{12,28},{16,0},{20,4},{24,8},{28,12},{1,17},{... | collective-permute-start | bytes 73736 | tf_op jit(solution)/shard_map/ppermute | solution.py:51
  259.8 16.4 %collective-permute-start.48 = (bf16[208,768]{1,0:T(8,128)(2,1)}, bf16[208,768]{1,0:T(8,128)(2,1)S(1)}, u32[]{:S(2)}, u32[]{:S(2)}) collective-permute-start(bf16[208,768]{1,0:T(8,128)(2,1)} %get-tuple-element.58), channel_id=1, source_target_pairs={{0,1},{1,0},{2,3},{3,2},{4,5},{5,4},{6,7},{7,6},{8,9},{9,8},{10,11... | collective-permute-start | bytes 958472 | tf_op jit(solution)/shard_map/ppermute | solution.py:51
  261.7 25.2 %collective-permute-start.49 = (bf16[208,768]{1,0:T(8,128)(2,1)}, bf16[208,768]{1,0:T(8,128)(2,1)S(1)}, u32[]{:S(2)}, u32[]{:S(2)}) collective-permute-start(bf16[208,768]{1,0:T(8,128)(2,1)} %get-tuple-element.59), channel_id=1, source_target_pairs={{0,2},{1,3},{2,0},{3,1},{4,6},{5,7},{6,4},{7,5},{8,10},{9,11},{10,... | collective-permute-start | bytes 958472 | tf_op jit(solution)/shard_map/ppermute | solution.py:51
  262.8 24.2 %collective-permute-start.50 = (bf16[208,768]{1,0:T(8,128)(2,1)S(1)}, bf16[208,768]{1,0:T(8,128)(2,1)S(1)}, u32[]{:S(2)}, u32[]{:S(2)}) collective-permute-start(bf16[208,768]{1,0:T(8,128)(2,1)S(1)} %copy-done.42), channel_id=1, source_target_pairs={{0,3},{1,2},{2,1},{3,0},{4,7},{5,6},{6,5},{7,4},{8,11},{9,10},{10,... | collective-permute-start | bytes 958472 | tf_op jit(solution)/shard_map/ppermute | solution.py:51
  276.1 15.1 %collective-permute-start.69 = (bf16[4,2,96,768]{3,2,1,0:T(8,128)(2,1)}, bf16[4,2,96,768]{3,2,1,0:T(8,128)(2,1)S(1)}, u32[]{:S(2)}, u32[]{:S(2)}) collective-permute-start(bf16[4,2,96,768]{3,2,1,0:T(8,128)(2,1)} %get-tuple-element.74), channel_id=1, source_target_pairs={{0,4},{4,0},{8,12},{12,8},{16,20},{20,16},{24,28},{28,24},{1,5},{5... | collective-permute-start | bytes 3538952 | tf_op jit(solution)/shard_map/ppermute | solution.py:51
  286.9 28.6 %collective-permute-start.56 = (bf16[4,8,96,384]{3,2,1,0:T(8,128)(2,1)S(1)}, bf16[4,8,96,384]{3,2,1,0:T(8,128)(2,1)S(1)}, u32[]{:S(2)}, u32[]{:S(2)}) collective-permute-start(bf16[4,8,96,384]{3,2,1,0:T(8,128)(2,1)S(1)} %copy-done.29), channel_id=1, source_target_pairs={{0,4},{4,0},{8,12},{12,8},{16,20},{20,16},{24,28},{28,24},{1,5},{5... | collective-permute-start | bytes 7077896 | tf_op jit(solution)/shard_map/ppermute | solution.py:51
  298.0 9.9 %collective-permute-start.78 = (bf16[2,96,768]{2,1,0:T(8,128)(2,1)S(1)}, bf16[2,96,768]{2,1,0:T(8,128)(2,1)S(1)}, u32[]{:S(2)}, u32[]{:S(2)}) collective-permute-start(bf16[2,96,768]{2,1,0:T(8,128)(2,1)S(1)} %pad_maximum_fusion.13), channel_id=1, source_target_pairs={{0,16},{4,20},{8,24},{12,28},{16,0},{20,4},{24,8},{28,12},{1,17},{... | collective-permute-start | bytes 884744 | tf_op jit(solution)/shard_map/ppermute | solution.py:51
  298.9 10.2 %collective-permute-start.76 = (bf16[2,96,768]{2,1,0:T(8,128)(2,1)S(1)}, bf16[2,96,768]{2,1,0:T(8,128)(2,1)S(1)}, u32[]{:S(2)}, u32[]{:S(2)}) collective-permute-start(bf16[2,96,768]{2,1,0:T(8,128)(2,1)S(1)} %pad_maximum_fusion.12), channel_id=1, source_target_pairs={{0,8},{4,12},{8,0},{12,4},{16,24},{20,28},{24,16},{28,20},{1,9},{5... | collective-permute-start | bytes 884744 | tf_op jit(solution)/shard_map/ppermute | solution.py:51
  301.6 12.7 %collective-permute-start.68 = (bf16[2,96,768]{2,1,0:T(8,128)(2,1)S(1)}, bf16[2,96,768]{2,1,0:T(8,128)(2,1)S(1)}, u32[]{:S(2)}, u32[]{:S(2)}) collective-permute-start(bf16[2,96,768]{2,1,0:T(8,128)(2,1)S(1)} %pad_maximum_fusion.9), channel_id=1, source_target_pairs={{0,16},{4,20},{8,24},{12,28},{16,0},{20,4},{24,8},{28,12},{1,17},{... | collective-permute-start | bytes 884744 | tf_op jit(solution)/shard_map/ppermute | solution.py:51
  302.5 13.0 %collective-permute-start.66 = (bf16[2,96,768]{2,1,0:T(8,128)(2,1)S(1)}, bf16[2,96,768]{2,1,0:T(8,128)(2,1)S(1)}, u32[]{:S(2)}, u32[]{:S(2)}) collective-permute-start(bf16[2,96,768]{2,1,0:T(8,128)(2,1)S(1)} %pad_maximum_fusion.8), channel_id=1, source_target_pairs={{0,8},{4,12},{8,0},{12,4},{16,24},{20,28},{24,16},{28,20},{1,9},{5... | collective-permute-start | bytes 884744 | tf_op jit(solution)/shard_map/ppermute | solution.py:51
  308.0 20.9 %collective-permute-start.73 = (bf16[2,96,768]{2,1,0:T(8,128)(2,1)S(1)}, bf16[2,96,768]{2,1,0:T(8,128)(2,1)S(1)}, u32[]{:S(2)}, u32[]{:S(2)}) collective-permute-start(bf16[2,96,768]{2,1,0:T(8,128)(2,1)S(1)} %pad_maximum_fusion.11), channel_id=1, source_target_pairs={{0,16},{4,20},{8,24},{12,28},{16,0},{20,4},{24,8},{28,12},{1,17},{... | collective-permute-start | bytes 884744 | tf_op jit(solution)/shard_map/ppermute | solution.py:51
  309.1 19.8 %collective-permute-start.71 = (bf16[2,96,768]{2,1,0:T(8,128)(2,1)S(1)}, bf16[2,96,768]{2,1,0:T(8,128)(2,1)S(1)}, u32[]{:S(2)}, u32[]{:S(2)}) collective-permute-start(bf16[2,96,768]{2,1,0:T(8,128)(2,1)S(1)} %pad_maximum_fusion.10), channel_id=1, source_target_pairs={{0,8},{4,12},{8,0},{12,4},{16,24},{20,28},{24,16},{28,20},{1,9},{5... | collective-permute-start | bytes 884744 | tf_op jit(solution)/shard_map/ppermute | solution.py:51
  316.1 10.5 %collective-permute-start.59 = (bf16[4,96,384]{2,1,0:T(8,128)(2,1)S(1)}, bf16[4,96,384]{2,1,0:T(8,128)(2,1)S(1)}, u32[]{:S(2)}, u32[]{:S(2)}) collective-permute-start(bf16[4,96,384]{2,1,0:T(8,128)(2,1)S(1)} %get-tuple-element.125), channel_id=1, source_target_pairs={{0,8},{4,12},{8,0},{12,4},{16,24},{20,28},{24,16},{28,20},{1,9},{5... | collective-permute-start | bytes 884744 | tf_op jit(solution)/shard_map/ppermute | solution.py:51
  316.8 11.2 %collective-permute-start.57 = (bf16[4,96,384]{2,1,0:T(8,128)(2,1)S(1)}, bf16[4,96,384]{2,1,0:T(8,128)(2,1)S(1)}, u32[]{:S(2)}, u32[]{:S(2)}) collective-permute-start(bf16[4,96,384]{2,1,0:T(8,128)(2,1)S(1)} %get-tuple-element.124), channel_id=1, source_target_pairs={{0,16},{4,20},{8,24},{12,28},{16,0},{20,4},{24,8},{28,12},{1,17},{... | collective-permute-start | bytes 884744 | tf_op jit(solution)/shard_map/ppermute | solution.py:51
  326.7 13.9 %collective-permute-start.60 = (bf16[8,96,384]{2,1,0:T(8,128)(2,1)S(1)}, bf16[8,96,384]{2,1,0:T(8,128)(2,1)S(1)}, u32[]{:S(2)}, u32[]{:S(2)}) collective-permute-start(bf16[8,96,384]{2,1,0:T(8,128)(2,1)S(1)} %pad_maximum_fusion.3), channel_id=1, source_target_pairs={{0,16},{4,20},{8,24},{12,28},{16,0},{20,4},{24,8},{28,12},{1,17},{... | collective-permute-start | bytes 1769480 | tf_op jit(solution)/shard_map/ppermute | solution.py:51
  328.2 13.6 %collective-permute-start.58 = (bf16[8,96,384]{2,1,0:T(8,128)(2,1)S(1)}, bf16[8,96,384]{2,1,0:T(8,128)(2,1)S(1)}, u32[]{:S(2)}, u32[]{:S(2)}) collective-permute-start(bf16[8,96,384]{2,1,0:T(8,128)(2,1)S(1)} %pad_maximum_fusion.2), channel_id=1, source_target_pairs={{0,8},{4,12},{8,0},{12,4},{16,24},{20,28},{24,16},{28,20},{1,9},{5... | collective-permute-start | bytes 1769480 | tf_op jit(solution)/shard_map/ppermute | solution.py:51
  348.2 9.2 %collective-permute-start.62 = (bf16[2,96,384]{2,1,0:T(8,128)(2,1)S(1)}, bf16[2,96,384]{2,1,0:T(8,128)(2,1)S(1)}, u32[]{:S(2)}, u32[]{:S(2)}) collective-permute-start(bf16[2,96,384]{2,1,0:T(8,128)(2,1)S(1)} %get-tuple-element.123), channel_id=1, source_target_pairs={{0,2},{1,3},{2,0},{3,1},{4,6},{5,7},{6,4},{7,5},{8,10},{9,11},{10,... | collective-permute-start | bytes 442376 | tf_op jit(solution)/shard_map/ppermute | solution.py:51
  (80 other events, 1290.2 us)
